TPU v7x, 32 devices: a whole 2x2x4 slice. The times are simulated.
32 devices in a mesh: dp: 8 (over z, y), group: 4 (over x, core).
Axes of the slice: x: 2, y: 2, z: 4, core: 2. Of those that a mesh axis runs over, the one named last changes fastest.
Arguments:
- queries: bfloat16 [4096, 2048], P(('dp', 'group')), may hold values from -100 to 100
- key_states: bfloat16 [4096, 512], P(('dp', 'group')), may hold values from -4 to 4
- value_states: bfloat16 [4096, 512], P(('dp', 'group')), may hold values from -6 to 6
- grad_out: bfloat16 [4096, 2048], P(('dp', 'group')), may hold values from -6 to 6
- doc_ids: int32 [4096], P(('dp', 'group')), may hold values from 0 to 5, never falling along the last dimension, each value on 1 to 896 neighbouring positions
Outputs:
- attended: bfloat16 [4096, 2048], P(('dp', 'group'))
- grad_queries: bfloat16 [4096, 2048], P(('dp', 'group'))
- grad_keys: bfloat16 [4096, 512], P(('dp', 'group'))
- grad_values: bfloat16 [4096, 512], P(('dp', 'group'))
Inputs may be any that keep to these rules, and one draw needn't show every extreme that they name: `doc_ids`: ids never fall along the window; every document holds 1 to 896 tokens, and some document exactly 896.
All inputs are finite; a program needn't handle non-finite values.
Results may differ from a plain program's by a relative error of at most 0.02.
Values may be sent and summed in bfloat16 or wider, within the bound.
No kernel may reach another device: no remote copies, remote signals or barrier semaphores. Data moves between devices by JAX's collectives and lax.ppermute only.
A program may use at most 64 MiB of HBM per device.

v0:
```python
import jax
import jax.numpy as jnp
from jax import lax
from jax.sharding import PartitionSpec as P

HEADS = 16
KV_HEADS = 4
HEAD = 128
WINDOW = 8


def passed_along(value, axis, steps):
    count = lax.axis_size(axis)
    leading, last = (max(0, -steps), min(count, count - steps))
    return lax.ppermute(value, axis, [(source, source + steps) for source in range(leading, last)])


def head_terms(query_head, key_head, value_head, grad_head, allowed):
    softmax_scale = HEAD ** (-0.5)
    scores = (
        jnp.einsum("igd,jd->gij", query_head, key_head, preferred_element_type=jnp.float32)
        * softmax_scale
    )
    scores = jnp.where(allowed[None], scores, -jnp.inf)
    row_max = jnp.max(scores, axis=-1, keepdims=True)
    log_total = row_max + jnp.log(jnp.sum(jnp.exp(scores - row_max), axis=-1, keepdims=True))
    weights = jnp.where(allowed[None], jnp.exp(scores - log_total), 0.0)
    probs_low = weights.astype(jnp.bfloat16)
    output = jnp.einsum(
        "gij,jd->igd", probs_low, value_head, preferred_element_type=jnp.float32
    ).astype(jnp.bfloat16)
    row_delta = jnp.sum(grad_head.astype(jnp.float32) * output.astype(jnp.float32), axis=-1)
    grad_probs = jnp.einsum(
        "igd,jd->gij", grad_head, value_head, preferred_element_type=jnp.float32
    )
    grad_scores = (weights * (grad_probs - row_delta.T[:, :, None]) * softmax_scale).astype(
        jnp.bfloat16
    )
    grad_query = jnp.einsum(
        "gij,jd->igd", grad_scores, key_head, preferred_element_type=jnp.float32
    ).astype(jnp.bfloat16)
    grad_key = jnp.einsum(
        "gij,igd->jd", grad_scores, query_head, preferred_element_type=jnp.float32
    )
    grad_value = jnp.einsum("gij,igd->jd", probs_low, grad_head, preferred_element_type=jnp.float32)
    return (output, grad_query, grad_key, grad_value)


def local(queries, key_states, value_states, grad_out, doc_ids):
    tok_rows = queries.shape[0]
    groups = HEADS // KV_HEADS
    device_rank = lax.axis_index(("dp", "group"))
    holding = (key_states[None], value_states[None], doc_ids[None])
    stride = 1
    while stride < WINDOW:
        arrived = passed_along((holding[0], holding[1], holding[2]), ("dp", "group"), stride)
        holding = (
            jnp.concatenate([holding[0], arrived[0]], 0),
            jnp.concatenate([holding[1], arrived[1]], 0),
            jnp.concatenate([holding[2], arrived[2]], 0),
        )
        stride = stride * 2
    key_stack, value_stack, id_stack = holding
    window_len = WINDOW * tok_rows
    key_index = jnp.arange(window_len, dtype=jnp.int32)
    distance_of = key_index // tok_rows
    key_place = (device_rank - distance_of) * tok_rows + key_index % tok_rows
    query_place = device_rank * tok_rows + jnp.arange(tok_rows, dtype=jnp.int32)
    allowed = (
        (id_stack.reshape(window_len)[None, :] == doc_ids[:, None])
        & (key_place[None, :] <= query_place[:, None])
        & (distance_of <= device_rank)[None, :]
    )
    query_heads = jnp.moveaxis(queries.reshape(tok_rows, KV_HEADS, groups, HEAD), 1, 0)
    grad_heads = jnp.moveaxis(grad_out.reshape(tok_rows, KV_HEADS, groups, HEAD), 1, 0)
    key_heads = jnp.moveaxis(key_stack.reshape(window_len, KV_HEADS, HEAD), 1, 0)
    value_heads = jnp.moveaxis(value_stack.reshape(window_len, KV_HEADS, HEAD), 1, 0)

    def per_head(operands):
        return head_terms(operands[0], operands[1], operands[2], operands[3], allowed)

    output, grad_query, grad_key, grad_value = lax.map(
        per_head, (query_heads, key_heads, value_heads, grad_heads)
    )
    attended = jnp.moveaxis(output, 0, 1).reshape(tok_rows, HEADS * HEAD)
    grad_queries = jnp.moveaxis(grad_query, 0, 1).reshape(tok_rows, HEADS * HEAD)
    key_terms = jnp.moveaxis(grad_key, 0, 1).reshape(WINDOW, tok_rows, KV_HEADS * HEAD)
    value_terms = jnp.moveaxis(grad_value, 0, 1).reshape(WINDOW, tok_rows, KV_HEADS * HEAD)
    totals = (key_terms, value_terms)
    half_len = WINDOW // 2
    while half_len >= 1:
        arrived = passed_along(
            (totals[0][half_len:], totals[1][half_len:]), ("dp", "group"), -half_len
        )
        totals = (totals[0][:half_len] + arrived[0], totals[1][:half_len] + arrived[1])
        half_len = half_len // 2
    totals = (totals[0][0], totals[1][0])
    return (attended, grad_queries, totals[0].astype(jnp.bfloat16), totals[1].astype(jnp.bfloat16))


def solution(mesh):
    placed = (
        P(("dp", "group"), None),
        P(("dp", "group"), None),
        P(("dp", "group"), None),
        P(("dp", "group"), None),
        P(("dp", "group")),
    )
    return jax.shard_map(
        local,
        mesh=mesh,
        in_specs=placed,
        out_specs=(
            P(("dp", "group"), None),
            P(("dp", "group"), None),
            P(("dp", "group"), None),
            P(("dp", "group"), None),
        ),
        check_vma=False,
    )
```

profile of v0, /device:TPU:1, one launch (start us, length us, event | category | flops | bytes accessed | tf_op | source)
XLA Modules:
  0.0 174.6 jit_solution(9741964531461702176)
XLA Ops:
  0.7 4.6 %collective-permute-start = (bf16[1,128,512]{2,1,0:T(8,128)(2,1)}, bf16[1,128,512]{2,1,0:T(8,128)(2,1)S(1)}, u32[]{:S(2)}, u32[]{:S(2)}) collective-permute-start(bf16[1,128,512]{2,1,0:T(8,128)(2,1)} %bitcast.137), channel_id=1, source_target_pairs={{0,1},{1,2},{2,3},{3,4},{4,5},{5,6},{6,7},{7,8},{8,9},{9,10},{10,1... | collective-permute-start | bytes 393224 | tf_op jit(solution)/shard_map/ppermute | solution.py:15
  5.3 1.9 %collective-permute-start.6 = (bf16[1,128,512]{2,1,0:T(8,128)(2,1)}, bf16[1,128,512]{2,1,0:T(8,128)(2,1)S(1)}, u32[]{:S(2)}, u32[]{:S(2)}) collective-permute-start(bf16[1,128,512]{2,1,0:T(8,128)(2,1)} %bitcast.141), channel_id=1, source_target_pairs={{0,1},{1,2},{2,3},{3,4},{4,5},{5,6},{6,7},{7,8},{8,9},{9,10},{10,1... | collective-permute-start | bytes 393224 | tf_op jit(solution)/shard_map/ppermute | solution.py:15
  7.2 3.5 %collective-permute-start.3 = (s32[1,128]{1,0:T(1,128)}, s32[1,128]{1,0:T(1,128)S(1)}, u32[]{:S(2)}, u32[]{:S(2)}) collective-permute-start(s32[1,128]{1,0:T(1,128)} %bitcast.149), channel_id=1, source_target_pairs={{0,1},{1,2},{2,3},{3,4},{4,5},{5,6},{6,7},{7,8},{8,9},{9,10},{10,1... | collective-permute-start | bytes 1544 | tf_op jit(solution)/shard_map/ppermute | solution.py:15
  11.8 3.1 %collective-permute-start.1 = (bf16[2,128,512]{2,1,0:T(8,128)(2,1)S(1)}, bf16[2,128,512]{2,1,0:T(8,128)(2,1)S(1)}, u32[]{:S(2)}, u32[]{:S(2)}) collective-permute-start(bf16[2,128,512]{2,1,0:T(8,128)(2,1)S(1)} %pad_maximum_fusion.4), channel_id=1, source_target_pairs={{0,2},{1,3},{2,4},{3,5},{4,6},{5,7},{6,8},{7,9},{8,10},{9,11},{10,... | collective-permute-start | bytes 786440 | tf_op jit(solution)/shard_map/ppermute | solution.py:15
  15.9 3.1 %collective-permute-start.7 = (bf16[2,128,512]{2,1,0:T(8,128)(2,1)S(1)}, bf16[2,128,512]{2,1,0:T(8,128)(2,1)S(1)}, u32[]{:S(2)}, u32[]{:S(2)}) collective-permute-start(bf16[2,128,512]{2,1,0:T(8,128)(2,1)S(1)} %pad_maximum_fusion.5), channel_id=1, source_target_pairs={{0,2},{1,3},{2,4},{3,5},{4,6},{5,7},{6,8},{7,9},{8,10},{9,11},{10,... | collective-permute-start | bytes 786440 | tf_op jit(solution)/shard_map/ppermute | solution.py:15
  19.7 3.2 %collective-permute-start.4 = (s32[2,128]{1,0:T(2,128)S(1)}, s32[2,128]{1,0:T(2,128)S(1)}, u32[]{:S(2)}, u32[]{:S(2)}) collective-permute-start(s32[2,128]{1,0:T(2,128)S(1)} %pad_add_fusion.1), channel_id=1, source_target_pairs={{0,2},{1,3},{2,4},{3,5},{4,6},{5,7},{6,8},{7,9},{8,10},{9,11},{10,... | collective-permute-start | bytes 3080 | tf_op jit(solution)/shard_map/ppermute | solution.py:15
  23.9 4.0 %collective-permute-start.2 = (bf16[4,128,512]{2,1,0:T(8,128)(2,1)S(1)}, bf16[4,128,512]{2,1,0:T(8,128)(2,1)}, u32[]{:S(2)}, u32[]{:S(2)}) collective-permute-start(bf16[4,128,512]{2,1,0:T(8,128)(2,1)S(1)} %pad_maximum_fusion.2), channel_id=1, source_target_pairs={{0,4},{1,5},{2,6},{3,7},{4,8},{5,9},{6,10},{7,11},{8,12},{9,13},{1... | collective-permute-start | bytes 1572872 | tf_op jit(solution)/shard_map/ppermute | solution.py:15
  28.7 3.8 %collective-permute-start.8 = (bf16[4,128,512]{2,1,0:T(8,128)(2,1)}, bf16[4,128,512]{2,1,0:T(8,128)(2,1)}, u32[]{:S(2)}, u32[]{:S(2)}) collective-permute-start(bf16[4,128,512]{2,1,0:T(8,128)(2,1)} %pad_maximum_fusion.3), channel_id=1, source_target_pairs={{0,4},{1,5},{2,6},{3,7},{4,8},{5,9},{6,10},{7,11},{8,12},{9,13},{1... | collective-permute-start | bytes 1572872 | tf_op jit(solution)/shard_map/ppermute | solution.py:15
  32.6 3.8 %collective-permute-start.5 = (s32[4,128]{1,0:T(4,128)S(1)}, s32[4,128]{1,0:T(4,128)S(1)}, u32[]{:S(2)}, u32[]{:S(2)}) collective-permute-start(s32[4,128]{1,0:T(4,128)S(1)} %pad_add_fusion), channel_id=1, source_target_pairs={{0,4},{1,5},{2,6},{3,7},{4,8},{5,9},{6,10},{7,11},{8,12},{9,13},{1... | collective-permute-start | bytes 6152 | tf_op jit(solution)/shard_map/ppermute | solution.py:15
  37.0 12.8 %collective-permute-done.5 = s32[4,128]{1,0:T(4,128)S(1)} collective-permute-done((s32[4,128]{1,0:T(4,128)S(1)}, s32[4,128]{1,0:T(4,128)S(1)}, u32[]{:S(2)}, u32[]{:S(2)}) %collective-permute-start.5) | collective-permute-done | bytes 2080 | tf_op jit(solution)/shard_map/ppermute | solution.py:15
  51.4 1.5 copy.47
  54.6 28.4 %while.17 = (s32[]{:T(128)}, bf16[4,128,4,128]{1,3,2,0:T(8,128)(2,1)}, bf16[4,128,4,128]{1,3,2,0:T(8,128)(2,1)}, f32[4,1024,128]{2,1,0:T(8,128)}, f32[4,1024,128...) while((s32[]{:T(128)}, ...), condition=%wide.region_4.5_spmd.clone, body=%wide.region_0.4_spmd.clone.sunk | while | flops 815135744 | bytes 21797036 | solution.py:82
  56.2 1.3 fusion.81
  59.5 1.2 fusion.80
  63.3 1.3 fusion.81
  77.5 1.2 fusion.81
  80.8 1.3 fusion.80
  83.0 1.7 fusion.52
  85.4 1.4 slice.59
  86.8 1.3 collective-permute-start.12
  88.1 2.7 %fusion.53 = (f32[512,4,128]{2,0,1:T(8,128)S(1)}, f32[512,4,128]{2,0,1:T(8,128)}) fusion(f32[1024,4,128]{2,0,1:T(8,128)} %bitcast.15), kind=kLoop, calls=%fused_computation.81 | loop fusion | bytes 4194304 | tf_op jit(solution)/shard_map/slice | solution.py:93
  91.4 1.4 slice.51
  92.8 1.3 collective-permute-start.9
  95.2 18.9 %collective-permute-done.12 = f32[4,128,512]{2,1,0:T(8,128)S(1)} collective-permute-done((f32[4,128,512]{2,1,0:T(8,128)}, f32[4,128,512]{2,1,0:T(8,128)S(1)}, u32[]{:S(2)}, u32[]{:S(2)}) %collective-permute-start.12) | collective-permute-done | bytes 1048608 | tf_op jit(solution)/shard_map/ppermute | solution.py:15
  115.2 1.3 collective-permute-start.13
  117.6 19.1 %collective-permute-done.9 = f32[4,128,512]{2,1,0:T(8,128)} collective-permute-done((f32[4,128,512]{2,1,0:T(8,128)}, f32[4,128,512]{2,1,0:T(8,128)}, u32[]{:S(2)}, u32[]{:S(2)}) %collective-permute-start.9) | collective-permute-done | bytes 1048608 | tf_op jit(solution)/shard_map/ppermute | solution.py:15
  136.7 1.4 add.72
  138.2 1.4 collective-permute-start.10
  140.8 3.2 %collective-permute-start.14 = (f32[1,128,512]{2,1,0:T(8,128)S(1)}, f32[1,128,512]{2,1,0:T(8,128)S(1)}, u32[]{:S(2)}, u32[]{:S(2)}) collective-permute-start(f32[1,128,512]{2,1,0:T(8,128)S(1)} %slice.75), channel_id=1, source_target_pairs={{1,0},{2,1},{3,2},{4,3},{5,4},{6,5},{7,6},{8,7},{9,8},{10,9},{11,1... | collective-permute-start | bytes 786440 | tf_op jit(solution)/shard_map/ppermute | solution.py:15
  144.0 19.9 %collective-permute-done.10 = f32[2,128,512]{2,1,0:T(8,128)S(1)} collective-permute-done((f32[2,128,512]{2,1,0:T(8,128)S(1)}, f32[2,128,512]{2,1,0:T(8,128)S(1)}, u32[]{:S(2)}, u32[]{:S(2)}) %collective-permute-start.10) | collective-permute-done | bytes 524320 | tf_op jit(solution)/shard_map/ppermute | solution.py:15
  163.9 3.6 %collective-permute-start.11 = (f32[1,128,512]{2,1,0:T(8,128)S(1)}, f32[1,128,512]{2,1,0:T(8,128)S(1)}, u32[]{:S(2)}, u32[]{:S(2)}) collective-permute-start(f32[1,128,512]{2,1,0:T(8,128)S(1)} %slice.69), channel_id=1, source_target_pairs={{1,0},{2,1},{3,2},{4,3},{5,4},{6,5},{7,6},{8,7},{9,8},{10,9},{11,1... | collective-permute-start | bytes 786440 | tf_op jit(solution)/shard_map/ppermute | solution.py:15
  170.3 3.6 %collective-permute-done.11 = f32[1,128,512]{2,1,0:T(8,128)S(1)} collective-permute-done((f32[1,128,512]{2,1,0:T(8,128)S(1)}, f32[1,128,512]{2,1,0:T(8,128)S(1)}, u32[]{:S(2)}, u32[]{:S(2)}) %collective-permute-start.11) | collective-permute-done | bytes 262176 | tf_op jit(solution)/shard_map/ppermute | solution.py:15
  (109 shorter events, 39.4 us)
Async XLA Ops:
  0.6 27.2 %copy-start.2 = (bf16[128,512]{1,0:T(8,128)(2,1)S(1)}, bf16[128,512]{1,0:T(8,128)(2,1)}, u32[]{:S(2)}) copy-start(bf16[128,512]{1,0:T(8,128)(2,1)} %param.8) | copy-start | bytes 393220
  0.6 31.9 %copy-start.9 = (s32[128]{0:T(128)S(1)}, s32[128]{0:T(128)}, u32[]{:S(2)}) copy-start(s32[128]{0:T(128)} %param.11) | copy-start | bytes 1540
  0.7 35.8 %copy-start.5 = (bf16[128,2048]{1,0:T(8,128)(2,1)S(1)}, bf16[128,2048]{1,0:T(8,128)(2,1)}, u32[]{:S(2)}) copy-start(bf16[128,2048]{1,0:T(8,128)(2,1)} %param.7) | copy-start | bytes 1572868
  0.7 10.1 %collective-permute-start = (bf16[1,128,512]{2,1,0:T(8,128)(2,1)}, bf16[1,128,512]{2,1,0:T(8,128)(2,1)S(1)}, u32[]{:S(2)}, u32[]{:S(2)}) collective-permute-start(bf16[1,128,512]{2,1,0:T(8,128)(2,1)} %bitcast.137), channel_id=1, source_target_pairs={{0,1},{1,2},{2,3},{3,4},{4,5},{5,6},{6,7},{7,8},{8,9},{9,10},{10,1... | collective-permute-start | bytes 393224 | tf_op jit(solution)/shard_map/ppermute | solution.py:15
  5.3 9.6 %collective-permute-start.6 = (bf16[1,128,512]{2,1,0:T(8,128)(2,1)}, bf16[1,128,512]{2,1,0:T(8,128)(2,1)S(1)}, u32[]{:S(2)}, u32[]{:S(2)}) collective-permute-start(bf16[1,128,512]{2,1,0:T(8,128)(2,1)} %bitcast.141), channel_id=1, source_target_pairs={{0,1},{1,2},{2,3},{3,4},{4,5},{5,6},{6,7},{7,8},{8,9},{9,10},{10,1... | collective-permute-start | bytes 393224 | tf_op jit(solution)/shard_map/ppermute | solution.py:15
  7.2 11.8 %collective-permute-start.3 = (s32[1,128]{1,0:T(1,128)}, s32[1,128]{1,0:T(1,128)S(1)}, u32[]{:S(2)}, u32[]{:S(2)}) collective-permute-start(s32[1,128]{1,0:T(1,128)} %bitcast.149), channel_id=1, source_target_pairs={{0,1},{1,2},{2,3},{3,4},{4,5},{5,6},{6,7},{7,8},{8,9},{9,10},{10,1... | collective-permute-start | bytes 1544 | tf_op jit(solution)/shard_map/ppermute | solution.py:15
  10.8 26.0 %copy-start.6 = (bf16[128,2048]{1,0:T(8,128)(2,1)S(1)}, bf16[128,2048]{1,0:T(8,128)(2,1)}, u32[]{:S(2)}) copy-start(bf16[128,2048]{1,0:T(8,128)(2,1)} %param.10) | copy-start | bytes 1572868
  11.8 11.1 %collective-permute-start.1 = (bf16[2,128,512]{2,1,0:T(8,128)(2,1)S(1)}, bf16[2,128,512]{2,1,0:T(8,128)(2,1)S(1)}, u32[]{:S(2)}, u32[]{:S(2)}) collective-permute-start(bf16[2,128,512]{2,1,0:T(8,128)(2,1)S(1)} %pad_maximum_fusion.4), channel_id=1, source_target_pairs={{0,2},{1,3},{2,4},{3,5},{4,6},{5,7},{6,8},{7,9},{8,10},{9,11},{10,... | collective-permute-start | bytes 786440 | tf_op jit(solution)/shard_map/ppermute | solution.py:15
  15.9 12.0 %collective-permute-start.7 = (bf16[2,128,512]{2,1,0:T(8,128)(2,1)S(1)}, bf16[2,128,512]{2,1,0:T(8,128)(2,1)S(1)}, u32[]{:S(2)}, u32[]{:S(2)}) collective-permute-start(bf16[2,128,512]{2,1,0:T(8,128)(2,1)S(1)} %pad_maximum_fusion.5), channel_id=1, source_target_pairs={{0,2},{1,3},{2,4},{3,5},{4,6},{5,7},{6,8},{7,9},{8,10},{9,11},{10,... | collective-permute-start | bytes 786440 | tf_op jit(solution)/shard_map/ppermute | solution.py:15
  19.7 30.2 %copy-start.1 = (bf16[128,512]{1,0:T(8,128)(2,1)S(1)}, bf16[128,512]{1,0:T(8,128)(2,1)}, u32[]{:S(2)}) copy-start(bf16[128,512]{1,0:T(8,128)(2,1)} %param.9) | copy-start | bytes 393220
  19.7 12.9 %collective-permute-start.4 = (s32[2,128]{1,0:T(2,128)S(1)}, s32[2,128]{1,0:T(2,128)S(1)}, u32[]{:S(2)}, u32[]{:S(2)}) collective-permute-start(s32[2,128]{1,0:T(2,128)S(1)} %pad_add_fusion.1), channel_id=1, source_target_pairs={{0,2},{1,3},{2,4},{3,5},{4,6},{5,7},{6,8},{7,9},{8,10},{9,11},{10,... | collective-permute-start | bytes 3080 | tf_op jit(solution)/shard_map/ppermute | solution.py:15
  23.9 26.0 %collective-permute-start.2 = (bf16[4,128,512]{2,1,0:T(8,128)(2,1)S(1)}, bf16[4,128,512]{2,1,0:T(8,128)(2,1)}, u32[]{:S(2)}, u32[]{:S(2)}) collective-permute-start(bf16[4,128,512]{2,1,0:T(8,128)(2,1)S(1)} %pad_maximum_fusion.2), channel_id=1, source_target_pairs={{0,4},{1,5},{2,6},{3,7},{4,8},{5,9},{6,10},{7,11},{8,12},{9,13},{1... | collective-permute-start | bytes 1572872 | tf_op jit(solution)/shard_map/ppermute | solution.py:15
  27.8 22.1 %copy-start.4 = (bf16[2,128,512]{2,1,0:T(8,128)(2,1)}, bf16[2,128,512]{2,1,0:T(8,128)(2,1)S(1)}, u32[]{:S(2)}) copy-start(bf16[2,128,512]{2,1,0:T(8,128)(2,1)S(1)} %collective-permute-done.7) | copy-start | bytes 786436
  28.7 24.2 %collective-permute-start.8 = (bf16[4,128,512]{2,1,0:T(8,128)(2,1)}, bf16[4,128,512]{2,1,0:T(8,128)(2,1)}, u32[]{:S(2)}, u32[]{:S(2)}) collective-permute-start(bf16[4,128,512]{2,1,0:T(8,128)(2,1)} %pad_maximum_fusion.3), channel_id=1, source_target_pairs={{0,4},{1,5},{2,6},{3,7},{4,8},{5,9},{6,10},{7,11},{8,12},{9,13},{1... | collective-permute-start | bytes 1572872 | tf_op jit(solution)/shard_map/ppermute | solution.py:15
  32.6 17.3 %collective-permute-start.5 = (s32[4,128]{1,0:T(4,128)S(1)}, s32[4,128]{1,0:T(4,128)S(1)}, u32[]{:S(2)}, u32[]{:S(2)}) collective-permute-start(s32[4,128]{1,0:T(4,128)S(1)} %pad_add_fusion), channel_id=1, source_target_pairs={{0,4},{1,5},{2,6},{3,7},{4,8},{5,9},{6,10},{7,11},{8,12},{9,13},{1... | collective-permute-start | bytes 6152 | tf_op jit(solution)/shard_map/ppermute | solution.py:15
  55.9 1.6 copy-start.3
  63.0 1.6 copy-start.3
  70.1 1.6 copy-start.3
  77.2 1.6 copy-start.3
  86.8 27.3 %collective-permute-start.12 = (f32[4,128,512]{2,1,0:T(8,128)}, f32[4,128,512]{2,1,0:T(8,128)S(1)}, u32[]{:S(2)}, u32[]{:S(2)}) collective-permute-start(f32[4,128,512]{2,1,0:T(8,128)} %slice.59), channel_id=1, source_target_pairs={{4,0},{5,1},{6,2},{7,3},{8,4},{9,5},{10,6},{11,7},{12,8},{13,9},{1... | collective-permute-start | bytes 3145736 | tf_op jit(solution)/shard_map/ppermute | solution.py:15
  92.8 43.9 %collective-permute-start.9 = (f32[4,128,512]{2,1,0:T(8,128)}, f32[4,128,512]{2,1,0:T(8,128)}, u32[]{:S(2)}, u32[]{:S(2)}) collective-permute-start(f32[4,128,512]{2,1,0:T(8,128)} %slice.51), channel_id=1, source_target_pairs={{4,0},{5,1},{6,2},{7,3},{8,4},{9,5},{10,6},{11,7},{12,8},{13,9},{1... | collective-permute-start | bytes 3145736 | tf_op jit(solution)/shard_map/ppermute | solution.py:15
  95.2 21.2 %copy-start = (f32[512,4,128]{2,0,1:T(8,128)S(1)}, f32[512,4,128]{2,0,1:T(8,128)}, u32[]{:S(2)}) copy-start(f32[512,4,128]{2,0,1:T(8,128)} %get-tuple-element.147) | copy-start | bytes 3145732
  115.2 24.5 %collective-permute-start.13 = (f32[2,128,512]{2,1,0:T(8,128)}, f32[2,128,512]{2,1,0:T(8,128)}, u32[]{:S(2)}, u32[]{:S(2)}) collective-permute-start(f32[2,128,512]{2,1,0:T(8,128)} %slice.73), channel_id=1, source_target_pairs={{2,0},{3,1},{4,2},{5,3},{6,4},{7,5},{8,6},{9,7},{10,8},{11,9},{12,... | collective-permute-start | bytes 1572872 | tf_op jit(solution)/shard_map/ppermute | solution.py:15
  138.2 29.4 %copy-start.7 = (bf16[4,128,4,128]{1,3,2,0:T(8,128)(2,1)S(1)}, bf16[4,128,4,128]{1,3,2,0:T(8,128)(2,1)}, u32[]{:S(2)}) copy-start(bf16[4,128,4,128]{1,3,2,0:T(8,128)(2,1)} %get-tuple-element.59) | copy-start | bytes 1572868
  138.2 25.6 %collective-permute-start.10 = (f32[2,128,512]{2,1,0:T(8,128)S(1)}, f32[2,128,512]{2,1,0:T(8,128)S(1)}, u32[]{:S(2)}, u32[]{:S(2)}) collective-permute-start(f32[2,128,512]{2,1,0:T(8,128)S(1)} %slice.67), channel_id=1, source_target_pairs={{2,0},{3,1},{4,2},{5,3},{6,4},{7,5},{8,6},{9,7},{10,8},{11,9},{12,... | collective-permute-start | bytes 1572872 | tf_op jit(solution)/shard_map/ppermute | solution.py:15
  140.8 27.9 %copy-start.8 = (bf16[4,128,4,128]{1,3,2,0:T(8,128)(2,1)S(1)}, bf16[4,128,4,128]{1,3,2,0:T(8,128)(2,1)}, u32[]{:S(2)}) copy-start(bf16[4,128,4,128]{1,3,2,0:T(8,128)(2,1)} %get-tuple-element.60) | copy-start | bytes 1572868
  140.8 28.8 %collective-permute-start.14 = (f32[1,128,512]{2,1,0:T(8,128)S(1)}, f32[1,128,512]{2,1,0:T(8,128)S(1)}, u32[]{:S(2)}, u32[]{:S(2)}) collective-permute-start(f32[1,128,512]{2,1,0:T(8,128)S(1)} %slice.75), channel_id=1, source_target_pairs={{1,0},{2,1},{3,2},{4,3},{5,4},{6,5},{7,6},{8,7},{9,8},{10,9},{11,1... | collective-permute-start | bytes 786440 | tf_op jit(solution)/shard_map/ppermute | solution.py:15
  163.9 9.9 %collective-permute-start.11 = (f32[1,128,512]{2,1,0:T(8,128)S(1)}, f32[1,128,512]{2,1,0:T(8,128)S(1)}, u32[]{:S(2)}, u32[]{:S(2)}) collective-permute-start(f32[1,128,512]{2,1,0:T(8,128)S(1)} %slice.69), channel_id=1, source_target_pairs={{1,0},{2,1},{3,2},{4,3},{5,4},{6,5},{7,6},{8,7},{9,8},{10,9},{11,1... | collective-permute-start | bytes 786440 | tf_op jit(solution)/shard_map/ppermute | solution.py:15
where the time goes:
time: 175 us
  waiting for transfers between devices  74.3 us (42%)
  starting transfers between devices  43.2 us (25%)
  matrix products  23.4 us (13%)
  local copies, waits for them, and re-layouts  16.5 us (9%)
  other arithmetic  16 us (9%)
    ppermute x15, waiting for transfers between devices, passed_along(): lax.ppermute(value, axis, [(source, source + steps) for source in range(l...  74.3 us
    ppermute x15, starting transfers between devices, passed_along(): lax.ppermute(value, axis, [(source, source + steps) for source in range(l...  43.2 us
    dot_general x4, matrix products, head_terms(): jnp.einsum('gij,igd->jd', probs_low, grad_head, preferred_element_type=jn...  5.01 us
    dot_general x4, matrix products, head_terms(): jnp.einsum('gij,igd->jd', grad_scores, query_head, preferred_element_type...  4.99 us
    slice x5, local copies, waits for them, and re-layouts, local(): totals[0][half_len:]  4.81 us
    slice x5, local copies, waits for them, and re-layouts, local(): totals[1][half_len:]  4.61 us
    dot_general x4, matrix products, head_terms(): jnp.einsum('gij,jd->igd', probs_low, value_head, preferred_element_type=j...  4.54 us
    dot_general x4, matrix products, head_terms(): jnp.einsum('gij,jd->igd', grad_scores, key_head, preferred_element_type=j...  3.96 us
  transfers between devices with their start and end apart: 15, of which 5 were waited for; matrix products, arithmetic and copies ran while one was open for 12% of the time, Pallas kernels for 0%

commit v1 on v0

v1 whole, which is shorter than its diff:
```python
import functools

import jax
import jax.numpy as jnp
from jax import lax
from jax.experimental import pallas as pl
from jax.experimental.pallas import tpu as pltpu
from jax.sharding import PartitionSpec as P

HEADS = 16
KV_HEADS = 4
HEAD = 128
WINDOW = 8
AXES = ("dp", "group")
GROUPS = HEADS // KV_HEADS
EXTRA = 16
PAIR = 2

VMEM = pl.BlockSpec(memory_space=pltpu.VMEM)
SMEM = pl.BlockSpec(memory_space=pltpu.SMEM)
BF16 = jnp.bfloat16
F32 = jnp.float32


def rows_at(index, rows):
    return pl.ds(pl.multiple_of(index * rows, rows), rows)


def call(kernel, name, outs, operands, scratch=()):
    return pl.pallas_call(
        kernel,
        out_shape=[jax.ShapeDtypeStruct(shape, dtype) for shape, dtype in outs],
        in_specs=[SMEM] + [VMEM] * (len(operands) - 1),
        out_specs=[VMEM] * len(outs),
        scratch_shapes=list(scratch),
        compiler_params=pltpu.CompilerParams(vmem_limit_bytes=48 * 1024 * 1024),
        name=name,
    )(*operands)


def pack_keys(tok, info, ids, keys, values, *slots):
    me = info[0]
    along = jnp.broadcast_to(ids[...], (tok, tok)).astype(F32)
    down = along.T
    local_start = jnp.sum((down < along).astype(F32), axis=0, keepdims=True)
    low = (ids[...] & 255).astype(F32)
    high = (ids[...] >> 8).astype(F32)
    marks = jnp.concatenate(
        [local_start, low, high, jnp.zeros((EXTRA - 3, tok), F32)], 0
    ).astype(BF16)
    for s, slot in enumerate(slots):
        columns = rows_at(me ^ s, HEAD)
        slot[0:tok, :] = keys[:, columns]
        slot[tok : 2 * tok, :] = values[:, columns]
        slot[2 * tok : 2 * tok + EXTRA, :] = marks


def pack_queries(tok, info, queries, grads, *slots):
    me = info[0]
    for s, slot in enumerate(slots):
        columns = rows_at(me ^ s, GROUPS * HEAD)
        slot[0:tok, :] = queries[:, columns]
        slot[tok : 2 * tok, :] = grads[:, columns]


def order_keys(tok, info, s0, s1, s2, s3, near, far):
    me = info[0]
    n = KV_HEADS
    for s, slot in enumerate((s0, s1, s2, s3)):
        block = me ^ s
        near[rows_at(block, tok), :] = slot[0:tok, :]
        near[rows_at(n + block, tok), :] = slot[tok : 2 * tok, :]
        near[pl.ds(pl.multiple_of(2 * n * tok + block * EXTRA, EXTRA), EXTRA), :] = slot[
            2 * tok : 2 * tok + EXTRA, :
        ]
    far[0 : 3 * tok, :] = near[tok : n * tok, :]
    far[3 * tok : 6 * tok, :] = near[(n + 1) * tok : 2 * n * tok, :]
    far[6 * tok :, :] = near[2 * n * tok + EXTRA :, :]


def attend(
    tok, info, own, near, far, q0, q1, q2, q3,
    r0, r1, r2, r3, own_terms, near_terms, far_terms,
    key_rows, value_rows, key_cols, value_cols, query_rows, grad_rows, marks, grad_keys, grad_values,
):
    me, quad = info[0], info[1]
    n = KV_HEADS
    span = WINDOW * tok
    before = span - tok
    blocks = 3 * n - 1
    key_rows[0 : 3 * tok, :] = far[0 : 3 * tok, :]
    key_rows[3 * tok : 7 * tok, :] = near[0 : 4 * tok, :]
    key_rows[7 * tok :, :] = own[0 : 4 * tok, :]
    value_rows[0 : 3 * tok, :] = far[3 * tok : 6 * tok, :]
    value_rows[3 * tok : 7 * tok, :] = near[4 * tok : 8 * tok, :]
    value_rows[7 * tok :, :] = own[4 * tok : 8 * tok, :]
    for b in range(blocks):
        at = slice(b * tok, (b + 1) * tok)
        key_cols[:, at] = key_rows[at, :].T
        value_cols[:, at] = value_rows[at, :].T
        if b < 3:
            mark = far[6 * tok + b * EXTRA : 6 * tok + (b + 1) * EXTRA, :]
        elif b < 7:
            mark = near[8 * tok + (b - 3) * EXTRA : 8 * tok + (b - 2) * EXTRA, :]
        else:
            mark = own[8 * tok + (b - 7) * EXTRA : 8 * tok + (b - 6) * EXTRA, :]
        mark = mark.astype(F32)
        ids = mark[1:2] + 256.0 * mark[2:3]
        exists = (quad - 2) * n + b + 1 >= 0
        marks[b : b + 1, :] = jnp.where(exists, ids, -1.0)
        if b >= 7:
            marks[16 + b - 7 : 17 + b - 7, :] = mark[0:1]
    for b in range(blocks, 16):
        marks[b : b + 1, :] = jnp.full((1, tok), -1.0, F32)
    for s, slot in enumerate((q0, q1, q2, q3)):
        for h in range(GROUPS):
            at = slice(h * tok, (h + 1) * tok)
            query_rows[s, at, :] = slot[0:tok, h * HEAD : (h + 1) * HEAD]
            grad_rows[s, at, :] = slot[tok : 2 * tok, h * HEAD : (h + 1) * HEAD]
    grad_keys[...] = jnp.zeros_like(grad_keys)
    grad_values[...] = jnp.zeros_like(grad_values)
    scale = HEAD ** (-0.5)
    key_place = lax.broadcasted_iota(jnp.int32, (span, tok), 0)
    query_limit = before + lax.broadcasted_iota(jnp.int32, (1, tok), 1)
    mark_row = lax.broadcasted_iota(jnp.int32, (16, tok), 0)

    for s, result in enumerate((r0, r1, r2, r3)):
        block = me ^ s
        window = rows_at(block, tok)
        window = pl.ds(pl.multiple_of(block * tok, tok), span)
        all_ids = marks[0:16, :]
        first = jnp.min(marks[pl.ds(block + 7, 1), :], axis=1, keepdims=True)
        earlier = (mark_row >= block) & (mark_row < block + 7) & (all_ids < first)
        count = jnp.sum(
            jnp.sum(earlier.astype(F32), axis=1, keepdims=True), axis=0, keepdims=True
        )
        local_start = marks[pl.ds(16 + block, 1), :]
        start = jnp.where(local_start == 0.0, count, before + local_start).astype(jnp.int32)
        allowed = (key_place >= start) & (key_place <= query_limit)
        bias = jnp.where(allowed, 0.0, -jnp.inf)
        bias = jnp.concatenate([bias] * PAIR, 1)

        def heads(i, carry):
            at = pl.ds(pl.multiple_of(i * PAIR * tok, PAIR * tok), PAIR * tok)
            query, grad = query_rows[s, at, :], grad_rows[s, at, :]
            scores = lax.dot_general(
                key_rows[window, :], query, (((1,), (1,)), ((), ())), preferred_element_type=F32
            )
            scores = scores + bias
            top = jnp.max(scores, axis=0, keepdims=True)
            weights = jnp.exp((scores - top) * scale)
            total = jnp.sum(weights, axis=0, keepdims=True)
            probs = weights * (1.0 / total)
            probs_low = probs.astype(BF16)
            output = jnp.dot(value_cols[:, window], probs_low, preferred_element_type=F32)
            output = output.astype(BF16).astype(F32)
            grad_probs = lax.dot_general(
                value_rows[window, :], grad, (((1,), (1,)), ((), ())), preferred_element_type=F32
            )
            grad_cols = jnp.concatenate(
                [grad[h * tok : (h + 1) * tok].T for h in range(PAIR)], 1
            ).astype(F32)
            delta = jnp.sum(grad_cols * output, axis=0, keepdims=True)
            grad_scores = (probs * (grad_probs - delta)).astype(BF16)
            grad_query = jnp.dot(key_cols[:, window], grad_scores, preferred_element_type=F32)
            grad_query = grad_query * scale
            grad_values[window, :] += jnp.dot(probs_low, grad, preferred_element_type=F32)
            grad_keys[window, :] += jnp.dot(grad_scores, query, preferred_element_type=F32)
            for h in range(PAIR):
                part = slice(h * tok, (h + 1) * tok)
                columns = pl.ds(pl.multiple_of((i * PAIR + h) * HEAD, HEAD), HEAD)
                result[0:tok, columns] = output[:, part].T.astype(BF16)
                result[tok : 2 * tok, columns] = grad_query[:, part].T.astype(BF16)
            return carry

        lax.fori_loop(0, GROUPS // PAIR, heads, 0)

    far_terms[0 : 3 * tok, :] = (grad_keys[0 : 3 * tok, :] * scale).astype(BF16)
    far_terms[3 * tok :, :] = grad_values[0 : 3 * tok, :].astype(BF16)
    near_terms[0 : 4 * tok, :] = (grad_keys[3 * tok : 7 * tok, :] * scale).astype(BF16)
    near_terms[4 * tok :, :] = grad_values[3 * tok : 7 * tok, :].astype(BF16)
    own_terms[0 : 4 * tok, :] = grad_keys[7 * tok :, :] * scale
    own_terms[4 * tok :, :] = grad_values[7 * tok :, :]


def add_terms(tok, info, own, near, far, s0, s1, s2, s3, total):
    me = info[0]
    n = KV_HEADS
    total[...] = own[...] + near[...].astype(F32)
    total[tok : n * tok, :] += far[0 : 3 * tok, :].astype(F32)
    total[(n + 1) * tok :, :] += far[3 * tok :, :].astype(F32)
    for s, slot in enumerate((s0, s1, s2, s3)):
        slot[0:tok, :] = total[rows_at(me ^ s, tok), :].astype(BF16)
        slot[tok : 2 * tok, :] = total[rows_at(n + (me ^ s), tok), :].astype(BF16)


def place_columns(tok, width, info, s0, s1, s2, s3, upper, lower):
    me = info[0]
    for s, slot in enumerate((s0, s1, s2, s3)):
        columns = rows_at(me ^ s, width)
        upper[:, columns] = slot[0:tok, :]
        lower[:, columns] = slot[tok : 2 * tok, :]


def local(queries, key_states, value_states, grad_out, doc_ids):
    tok = queries.shape[0]
    n = KV_HEADS
    count = lax.axis_size("dp") * lax.axis_size("group")
    rank = lax.axis_index(AXES)
    info = jnp.stack([rank % n, rank // n]).astype(jnp.int32)

    def swap(value, bits):
        return lax.ppermute(value, AXES, [(i, i ^ bits) for i in range(count)])

    def ring(value, steps):
        return lax.ppermute(value, AXES, [(i, (i + steps) % count) for i in range(count)])

    def exchange(slots):
        return [slots[0]] + [swap(slots[s], s) for s in range(1, n)]

    kv_slots = call(
        functools.partial(pack_keys, tok),
        "pack_keys",
        [((2 * tok + EXTRA, HEAD), BF16)] * n,
        (info, doc_ids[None, :], key_states, value_states),
    )
    kv_slots = exchange(kv_slots)
    query_slots = call(
        functools.partial(pack_queries, tok),
        "pack_queries",
        [((2 * tok, GROUPS * HEAD), BF16)] * n,
        (info, queries, grad_out),
    )
    query_slots = exchange(query_slots)
    own, own_late = call(
        functools.partial(order_keys, tok),
        "order_keys",
        [((2 * n * tok + n * EXTRA, HEAD), BF16), ((6 * tok + 3 * EXTRA, HEAD), BF16)],
        (info, *kv_slots),
    )
    near = ring(own, n)
    far = ring(own_late, 2 * n)
    blocks = 3 * n - 1
    results = call(
        functools.partial(attend, tok),
        "attend",
        [((2 * tok, GROUPS * HEAD), BF16)] * n
        + [((2 * n * tok, HEAD), F32), ((2 * n * tok, HEAD), BF16), ((6 * tok, HEAD), BF16)],
        (info, own, near, far, *query_slots),
        [
            pltpu.VMEM((blocks * tok, HEAD), BF16),
            pltpu.VMEM((blocks * tok, HEAD), BF16),
            pltpu.VMEM((HEAD, blocks * tok), BF16),
            pltpu.VMEM((HEAD, blocks * tok), BF16),
            pltpu.VMEM((n, GROUPS * tok, HEAD), BF16),
            pltpu.VMEM((n, GROUPS * tok, HEAD), BF16),
            pltpu.VMEM((24, tok), F32),
            pltpu.VMEM((blocks * tok, HEAD), F32),
            pltpu.VMEM((blocks * tok, HEAD), F32),
        ],
    )
    out_slots, (own_terms, near_terms, far_terms) = results[:n], results[n:]
    near_back = ring(near_terms, -n)
    far_back = ring(far_terms, -2 * n)
    out_slots = exchange(out_slots)
    grad_slots = call(
        functools.partial(add_terms, tok),
        "add_terms",
        [((2 * tok, HEAD), BF16)] * n,
        (info, own_terms, near_back, far_back),
        [pltpu.VMEM((2 * n * tok, HEAD), F32)],
    )
    grad_slots = exchange(grad_slots)
    attended, grad_queries = call(
        functools.partial(place_columns, tok, GROUPS * HEAD),
        "place_queries",
        [((tok, HEADS * HEAD), BF16)] * 2,
        (info, *out_slots),
    )
    grad_keys, grad_values = call(
        functools.partial(place_columns, tok, HEAD),
        "place_keys",
        [((tok, KV_HEADS * HEAD), BF16)] * 2,
        (info, *grad_slots),
    )
    return (attended, grad_queries, grad_keys, grad_values)


def solution(mesh):
    rows = P(AXES, None)
    return jax.shard_map(
        local,
        mesh=mesh,
        in_specs=(rows, rows, rows, rows, P(AXES)),
        out_specs=(rows, rows, rows, rows),
        check_vma=False,
    )
```

time: 175 us -> 67.3 us (0.38)
  waiting for transfers between devices: 74.3 us -> 24.2 us
  starting transfers between devices: 43.2 us -> 17.7 us
  matrix products: 23.4 us -> 0 us
  Pallas kernels: 0 us -> 20.8 us
  other arithmetic: 16 us -> 0.08 us
  local copies, waits for them, and re-layouts: 16.5 us -> 3.56 us
    ppermute x15 -> x16, waiting for transfers between devices: 74.3 us -> 24.2 us  [the longest x12 18.2 us: swap(): return lax.ppermute(value, AXES, [(i, i ^ bits) for i in range(count)])]
    ppermute x15 -> x16, starting transfers between devices: 43.2 us -> 17.7 us  [the longest x12 10.5 us: swap(): return lax.ppermute(value, AXES, [(i, i ^ bits) for i in range(count)])]
    dot_general x24 -> x0, matrix products: 23.4 us -> none  [the longest x4 5.01 us: head_terms(): jnp.einsum('gij,igd->jd', probs_low, grad_head, preferred_element_type=jn...]
    pallas_call x0 -> x7, Pallas kernels: none -> 20.8 us  [call(): pl.pallas_call(kernel, out_shape=[jax.ShapeDtypeStruct(shape, dtype) for...]
    slice x14 -> x0, local copies, waits for them, and re-layouts: 11.6 us -> none  [the longest x5 4.81 us: local(): totals[0][half_len:]]
    concatenate x8 -> x0, other arithmetic: 6.79 us -> none  [the longest x3 3.09 us: local(): jnp.concatenate([holding[1], arrived[1]], 0)]
    reshape x5 -> x0, local copies, waits for them, and re-layouts: 4.12 us -> none  [the longest x2 1.82 us: local(): value_stack.reshape(window_len, KV_HEADS, HEAD)]
    and x4 -> x0, other arithmetic: 3.48 us -> none  [local(): (id_stack.reshape(window_len)[None, :] == doc_ids[:, None]) & (key_place[...]
  transfers between devices with their start and end apart: 15 -> 16, of which waited for: 5 -> 7; matrix products, arithmetic and copies ran while one was open for 12% -> 0% of each run, Pallas kernels for 0% -> 4%
where the time goes in v1:
time: 67.3 us; the launch traced here: 67.1 us
  waiting for transfers between devices  24.2 us (36%)
  Pallas kernels  20.8 us (31%)
  starting transfers between devices  17.7 us (26%)
  local copies, waits for them, and re-layouts  3.56 us (5%)
  between operations  0.71 us (1%)
    pallas_call x7, Pallas kernels, call(): pl.pallas_call(kernel, out_shape=[jax.ShapeDtypeStruct(shape, dtype) for...  20.8 us
    ppermute x12, waiting for transfers between devices, swap(): return lax.ppermute(value, AXES, [(i, i ^ bits) for i in range(count)])  18.2 us
    ppermute x12, starting transfers between devices, swap(): return lax.ppermute(value, AXES, [(i, i ^ bits) for i in range(count)])  10.5 us
    ppermute x4, starting transfers between devices, ring(): lax.ppermute(value, AXES, [(i, (i + steps) % count) for i in range(count)])  7.14 us
    ppermute x4, waiting for transfers between devices, ring(): lax.ppermute(value, AXES, [(i, (i + steps) % count) for i in range(count)])  5.97 us
    unnamed x10, local copies, waits for them, and re-layouts  3.56 us
  transfers between devices with their start and end apart: 16, of which 7 were waited for; matrix products, arithmetic and copies ran while one was open for 0% of the time, Pallas kernels for 4%

profile of v1, /device:TPU:1, one launch (start us, length us, event | category | flops | bytes accessed | tf_op | source)
XLA Modules:
  0.0 67.1 jit_solution(15879438562772853019)
XLA Ops:
  0.7 1.0 %copy-done.2 = bf16[128,512]{1,0:T(8,128)(2,1)S(1)} copy-done((bf16[128,512]{1,0:T(8,128)(2,1)S(1)}, bf16[128,512]{1,0:T(8,128)(2,1)}, u32[]{:S(2)}) %copy-start.2) | copy-done | bytes 131096
  1.7 0.9 %copy-done.3 = bf16[128,512]{1,0:T(8,128)(2,1)S(1)} copy-done((bf16[128,512]{1,0:T(8,128)(2,1)S(1)}, bf16[128,512]{1,0:T(8,128)(2,1)}, u32[]{:S(2)}) %copy-start.3) | copy-done | bytes 131096
  2.6 0.7 copy-done.4
  3.3 0.7 pack_keys.1
  4.0 2.7 %collective-permute-start.1 = (bf16[272,128]{1,0:T(8,128)(2,1)S(1)}, bf16[272,128]{1,0:T(8,128)(2,1)S(1)}, u32[]{:S(2)}, u32[]{:S(2)}) collective-permute-start(bf16[272,128]{1,0:T(8,128)(2,1)S(1)} %get-tuple-element.31), channel_id=1, source_target_pairs={{0,2},{1,3},{2,0},{3,1},{4,6},{5,7},{6,4},{7,5},{8,10},{9,11},{10,... | collective-permute-start | bytes 208904 | tf_op jit(solution)/shard_map/ppermute | solution.py:213
  6.7 2.4 %collective-permute-done.1.s2 = bf16[272,128]{1,0:T(8,128)(2,1)S(1)} collective-permute-done((bf16[272,128]{1,0:T(8,128)(2,1)S(1)}, bf16[272,128]{1,0:T(8,128)(2,1)S(1)}, u32[]{:S(2)}, u32[]{:S(2)}) %collective-permute-start.1) | collective-permute-done | bytes 69664 | tf_op jit(solution)/shard_map/ppermute | solution.py:213
  9.2 1.7 %collective-permute-done.2.s3 = bf16[272,128]{1,0:T(8,128)(2,1)S(1)} collective-permute-done((bf16[272,128]{1,0:T(8,128)(2,1)S(1)}, bf16[272,128]{1,0:T(8,128)(2,1)S(1)}, u32[]{:S(2)}, u32[]{:S(2)}) %collective-permute-start.2) | collective-permute-done | bytes 69664 | tf_op jit(solution)/shard_map/ppermute | solution.py:213
  10.8 0.6 order_keys.1
  11.4 1.3 %collective-permute-start.3 = (bf16[1088,128]{1,0:T(8,128)(2,1)S(1)}, bf16[1088,128]{1,0:T(8,128)(2,1)S(1)}, u32[]{:S(2)}, u32[]{:S(2)}) collective-permute-start(bf16[1088,128]{1,0:T(8,128)(2,1)S(1)} %get-tuple-element.33.own), channel_id=1, source_target_pairs={{0,4},{1,5},{2,6},{3,7},{4,8},{5,9},{6,10},{7,11},{8,12},{9,13},{1... | collective-permute-start | bytes 835592 | tf_op jit(solution)/shard_map/ppermute | solution.py:216
  12.8 1.0 %copy-done.1 = bf16[128,2048]{1,0:T(8,128)(2,1)S(1)} copy-done((bf16[128,2048]{1,0:T(8,128)(2,1)S(1)}, bf16[128,2048]{1,0:T(8,128)(2,1)}, u32[]{:S(2)}) %copy-start.1) | copy-done | bytes 524312
  13.8 0.6 pack_queries.1
  14.4 0.7 %collective-permute-start.5 = (bf16[256,512]{1,0:T(8,128)(2,1)S(1)}, bf16[256,512]{1,0:T(8,128)(2,1)S(1)}, u32[]{:S(2)}, u32[]{:S(2)}) collective-permute-start(bf16[256,512]{1,0:T(8,128)(2,1)S(1)} %get-tuple-element.36), channel_id=1, source_target_pairs={{0,1},{1,0},{2,3},{3,2},{4,5},{5,4},{6,7},{7,6},{8,9},{9,8},{10,11... | collective-permute-start | bytes 786440 | tf_op jit(solution)/shard_map/ppermute | solution.py:213
  15.2 1.1 %collective-permute-start.6 = (bf16[256,512]{1,0:T(8,128)(2,1)S(1)}, bf16[256,512]{1,0:T(8,128)(2,1)S(1)}, u32[]{:S(2)}, u32[]{:S(2)}) collective-permute-start(bf16[256,512]{1,0:T(8,128)(2,1)S(1)} %get-tuple-element.37), channel_id=1, source_target_pairs={{0,2},{1,3},{2,0},{3,1},{4,6},{5,7},{6,4},{7,5},{8,10},{9,11},{10,... | collective-permute-start | bytes 786440 | tf_op jit(solution)/shard_map/ppermute | solution.py:213
  16.2 0.6 collective-permute-start.7
  16.9 1.3 %collective-permute-start.4 = (bf16[816,128]{1,0:T(8,128)(2,1)S(1)}, bf16[816,128]{1,0:T(8,128)(2,1)S(1)}, u32[]{:S(2)}, u32[]{:S(2)}) collective-permute-start(bf16[816,128]{1,0:T(8,128)(2,1)S(1)} %get-tuple-element.34), channel_id=1, source_target_pairs={{0,8},{1,9},{2,10},{3,11},{4,12},{5,13},{6,14},{7,15},{8,16},{9,17... | collective-permute-start | bytes 626696 | tf_op jit(solution)/shard_map/ppermute | solution.py:216
  18.2 4.9 %collective-permute-done.6.q2 = bf16[256,512]{1,0:T(8,128)(2,1)S(1)} collective-permute-done((bf16[256,512]{1,0:T(8,128)(2,1)S(1)}, bf16[256,512]{1,0:T(8,128)(2,1)S(1)}, u32[]{:S(2)}, u32[]{:S(2)}) %collective-permute-start.6) | collective-permute-done | bytes 262176 | tf_op jit(solution)/shard_map/ppermute | solution.py:213
  23.1 5.8 %collective-permute-done.7.q3 = bf16[256,512]{1,0:T(8,128)(2,1)S(1)} collective-permute-done((bf16[256,512]{1,0:T(8,128)(2,1)S(1)}, bf16[256,512]{1,0:T(8,128)(2,1)S(1)}, u32[]{:S(2)}, u32[]{:S(2)}) %collective-permute-start.7) | collective-permute-done | bytes 262176 | tf_op jit(solution)/shard_map/ppermute | solution.py:213
  28.8 15.4 %attend.1 = (bf16[256,512]{1,0:T(8,128)(2,1)S(1)}, bf16[256,512]{1,0:T(8,128)(2,1)S(1)}, bf16[256,512]{1,0:T(8,128)(2,1)S(1)}, bf16[256,512]{1,0:T(8,128)(2,1)S(...) custom-call(s32[2]{0:T(128)S(1)} %pad_add_fusion.info, ...), custom_call_target="tpu_custom_call" | custom-call | tf_op jit(solution)/shard_map/attend/pallas_call | solution.py:30
  44.3 2.9 %collective-permute-start.11 = (bf16[1024,128]{1,0:T(8,128)(2,1)S(1)}, bf16[1024,128]{1,0:T(8,128)(2,1)S(1)}, u32[]{:S(2)}, u32[]{:S(2)}) collective-permute-start(bf16[1024,128]{1,0:T(8,128)(2,1)S(1)} %get-tuple-element.46), channel_id=1, source_target_pairs={{0,28},{1,29},{2,30},{3,31},{4,0},{5,1},{6,2},{7,3},{8,4},{9,5},{1... | collective-permute-start | bytes 786440 | tf_op jit(solution)/shard_map/ppermute | solution.py:216
  47.2 0.5 collective-permute-start.8
  47.7 1.6 %collective-permute-start.12 = (bf16[768,128]{1,0:T(8,128)(2,1)S(1)}, bf16[768,128]{1,0:T(8,128)(2,1)S(1)}, u32[]{:S(2)}, u32[]{:S(2)}) collective-permute-start(bf16[768,128]{1,0:T(8,128)(2,1)S(1)} %get-tuple-element.47), channel_id=1, source_target_pairs={{0,24},{1,25},{2,26},{3,27},{4,28},{5,29},{6,30},{7,31},{8,0},{9,1... | collective-permute-start | bytes 589832 | tf_op jit(solution)/shard_map/ppermute | solution.py:216
  49.3 1.0 %collective-permute-start.9 = (bf16[256,512]{1,0:T(8,128)(2,1)S(1)}, bf16[256,512]{1,0:T(8,128)(2,1)S(1)}, u32[]{:S(2)}, u32[]{:S(2)}) collective-permute-start(bf16[256,512]{1,0:T(8,128)(2,1)S(1)} %get-tuple-element.41), channel_id=1, source_target_pairs={{0,2},{1,3},{2,0},{3,1},{4,6},{5,7},{6,4},{7,5},{8,10},{9,11},{10,... | collective-permute-start | bytes 786440 | tf_op jit(solution)/shard_map/ppermute | solution.py:213
  50.4 0.9 %collective-permute-start.10 = (bf16[256,512]{1,0:T(8,128)(2,1)S(1)}, bf16[256,512]{1,0:T(8,128)(2,1)S(1)}, u32[]{:S(2)}, u32[]{:S(2)}) collective-permute-start(bf16[256,512]{1,0:T(8,128)(2,1)S(1)} %get-tuple-element.42), channel_id=1, source_target_pairs={{0,3},{1,2},{2,1},{3,0},{4,7},{5,6},{6,5},{7,4},{8,11},{9,10},{10,... | collective-permute-start | bytes 786440 | tf_op jit(solution)/shard_map/ppermute | solution.py:213
  51.2 6.0 %collective-permute-done.12.far = bf16[768,128]{1,0:T(8,128)(2,1)S(1)} collective-permute-done((bf16[768,128]{1,0:T(8,128)(2,1)S(1)}, bf16[768,128]{1,0:T(8,128)(2,1)S(1)}, u32[]{:S(2)}, u32[]{:S(2)}) %collective-permute-start.12) | collective-permute-done | bytes 196640 | tf_op jit(solution)/shard_map/ppermute | solution.py:216
  57.2 0.7 add_terms.1
  57.9 1.1 %collective-permute-start.13 = (bf16[256,128]{1,0:T(8,128)(2,1)S(1)}, bf16[256,128]{1,0:T(8,128)(2,1)S(1)}, u32[]{:S(2)}, u32[]{:S(2)}) collective-permute-start(bf16[256,128]{1,0:T(8,128)(2,1)S(1)} %get-tuple-element.49), channel_id=1, source_target_pairs={{0,1},{1,0},{2,3},{3,2},{4,5},{5,4},{6,7},{7,6},{8,9},{9,8},{10,11... | collective-permute-start | bytes 196616 | tf_op jit(solution)/shard_map/ppermute | solution.py:213
  59.0 1.1 %collective-permute-start.14 = (bf16[256,128]{1,0:T(8,128)(2,1)S(1)}, bf16[256,128]{1,0:T(8,128)(2,1)S(1)}, u32[]{:S(2)}, u32[]{:S(2)}) collective-permute-start(bf16[256,128]{1,0:T(8,128)(2,1)S(1)} %get-tuple-element.50), channel_id=1, source_target_pairs={{0,2},{1,3},{2,0},{3,1},{4,6},{5,7},{6,4},{7,5},{8,10},{9,11},{10,... | collective-permute-start | bytes 196616 | tf_op jit(solution)/shard_map/ppermute | solution.py:213
  60.0 0.6 collective-permute-start.15
  60.7 3.0 %collective-permute-done.10.s3 = bf16[256,512]{1,0:T(8,128)(2,1)S(1)} collective-permute-done((bf16[256,512]{1,0:T(8,128)(2,1)S(1)}, bf16[256,512]{1,0:T(8,128)(2,1)S(1)}, u32[]{:S(2)}, u32[]{:S(2)}) %collective-permute-start.10) | collective-permute-done | bytes 262176 | tf_op jit(solution)/shard_map/ppermute | solution.py:213
  63.7 1.6 %place_queries.1 = (bf16[128,2048]{1,0:T(8,128)(2,1)}, bf16[128,2048]{1,0:T(8,128)(2,1)}) custom-call(s32[2]{0:T(128)S(1)} %pad_add_fusion.info, bf16[256,512]{1,0:T(8,128)(2,1)S(1)} %get-tuple-element.39.s0, bf16[256,512]{1,0:T(8,128)(2,1)S(1)} %collective-permute-done.8.s1, bf16[256,512]{1,0:T(8,128)(2,1)S(1)} %collective-permute-done.9.s2, ...), custom_call_target="tpu_custom_call" | custom-call | tf_op jit(solution)/shard_map/place_queries/pallas_call | solution.py:30
  65.3 0.5 collective-permute-done.15.s3
  65.8 1.3 %place_keys.1 = (bf16[128,512]{1,0:T(8,128)(2,1)}, bf16[128,512]{1,0:T(8,128)(2,1)}) custom-call(s32[2]{0:T(128)S(1)} %pad_add_fusion.info, bf16[256,128]{1,0:T(8,128)(2,1)S(1)} %get-tuple-element.48.s0, bf16[256,128]{1,0:T(8,128)(2,1)S(1)} %collective-permute-done.13.s1, bf16[256,128]{1,0:T(8,128)(2,1)S(1)} %collective-permute-done.14.s2, ...), custom_call_target="tpu_custom_call" | custom-call | tf_op jit(solution)/shard_map/place_keys/pallas_call | solution.py:30
  (18 shorter events, 0.3 us)
Async XLA Ops:
  0.6 12.1 %copy-start = (bf16[128,2048]{1,0:T(8,128)(2,1)S(1)}, bf16[128,2048]{1,0:T(8,128)(2,1)}, u32[]{:S(2)}) copy-start(bf16[128,2048]{1,0:T(8,128)(2,1)} %queries.1) | copy-start | bytes 1572868
  0.7 1.0 %copy-start.2 = (bf16[128,512]{1,0:T(8,128)(2,1)S(1)}, bf16[128,512]{1,0:T(8,128)(2,1)}, u32[]{:S(2)}) copy-start(bf16[128,512]{1,0:T(8,128)(2,1)} %keys.1) | copy-start | bytes 393220
  1.7 0.9 %copy-start.3 = (bf16[128,512]{1,0:T(8,128)(2,1)S(1)}, bf16[128,512]{1,0:T(8,128)(2,1)}, u32[]{:S(2)}) copy-start(bf16[128,512]{1,0:T(8,128)(2,1)} %values.1) | copy-start | bytes 393220
  2.6 0.7 copy-start.4
  3.9 2.8 %collective-permute-start = (bf16[272,128]{1,0:T(8,128)(2,1)S(1)}, bf16[272,128]{1,0:T(8,128)(2,1)S(1)}, u32[]{:S(2)}, u32[]{:S(2)}) collective-permute-start(bf16[272,128]{1,0:T(8,128)(2,1)S(1)} %get-tuple-element.30), channel_id=1, source_target_pairs={{0,1},{1,0},{2,3},{3,2},{4,5},{5,4},{6,7},{7,6},{8,9},{9,8},{10,11... | collective-permute-start | bytes 208904 | tf_op jit(solution)/shard_map/ppermute | solution.py:213
  4.0 5.1 %collective-permute-start.1 = (bf16[272,128]{1,0:T(8,128)(2,1)S(1)}, bf16[272,128]{1,0:T(8,128)(2,1)S(1)}, u32[]{:S(2)}, u32[]{:S(2)}) collective-permute-start(bf16[272,128]{1,0:T(8,128)(2,1)S(1)} %get-tuple-element.31), channel_id=1, source_target_pairs={{0,2},{1,3},{2,0},{3,1},{4,6},{5,7},{6,4},{7,5},{8,10},{9,11},{10,... | collective-permute-start | bytes 208904 | tf_op jit(solution)/shard_map/ppermute | solution.py:213
  6.7 4.1 %collective-permute-start.2 = (bf16[272,128]{1,0:T(8,128)(2,1)S(1)}, bf16[272,128]{1,0:T(8,128)(2,1)S(1)}, u32[]{:S(2)}, u32[]{:S(2)}) collective-permute-start(bf16[272,128]{1,0:T(8,128)(2,1)S(1)} %get-tuple-element.32), channel_id=1, source_target_pairs={{0,3},{1,2},{2,1},{3,0},{4,7},{5,6},{6,5},{7,4},{8,11},{9,10},{10,... | collective-permute-start | bytes 208904 | tf_op jit(solution)/shard_map/ppermute | solution.py:213
  11.4 17.4 %collective-permute-start.3 = (bf16[1088,128]{1,0:T(8,128)(2,1)S(1)}, bf16[1088,128]{1,0:T(8,128)(2,1)S(1)}, u32[]{:S(2)}, u32[]{:S(2)}) collective-permute-start(bf16[1088,128]{1,0:T(8,128)(2,1)S(1)} %get-tuple-element.33.own), channel_id=1, source_target_pairs={{0,4},{1,5},{2,6},{3,7},{4,8},{5,9},{6,10},{7,11},{8,12},{9,13},{1... | collective-permute-start | bytes 835592 | tf_op jit(solution)/shard_map/ppermute | solution.py:216
  12.8 1.0 %copy-start.1 = (bf16[128,2048]{1,0:T(8,128)(2,1)S(1)}, bf16[128,2048]{1,0:T(8,128)(2,1)}, u32[]{:S(2)}) copy-start(bf16[128,2048]{1,0:T(8,128)(2,1)} %grads.1) | copy-start | bytes 1572868
  14.4 3.7 %collective-permute-start.5 = (bf16[256,512]{1,0:T(8,128)(2,1)S(1)}, bf16[256,512]{1,0:T(8,128)(2,1)S(1)}, u32[]{:S(2)}, u32[]{:S(2)}) collective-permute-start(bf16[256,512]{1,0:T(8,128)(2,1)S(1)} %get-tuple-element.36), channel_id=1, source_target_pairs={{0,1},{1,0},{2,3},{3,2},{4,5},{5,4},{6,7},{7,6},{8,9},{9,8},{10,11... | collective-permute-start | bytes 786440 | tf_op jit(solution)/shard_map/ppermute | solution.py:213
  15.2 7.9 %collective-permute-start.6 = (bf16[256,512]{1,0:T(8,128)(2,1)S(1)}, bf16[256,512]{1,0:T(8,128)(2,1)S(1)}, u32[]{:S(2)}, u32[]{:S(2)}) collective-permute-start(bf16[256,512]{1,0:T(8,128)(2,1)S(1)} %get-tuple-element.37), channel_id=1, source_target_pairs={{0,2},{1,3},{2,0},{3,1},{4,6},{5,7},{6,4},{7,5},{8,10},{9,11},{10,... | collective-permute-start | bytes 786440 | tf_op jit(solution)/shard_map/ppermute | solution.py:213
  16.2 12.6 %collective-permute-start.7 = (bf16[256,512]{1,0:T(8,128)(2,1)S(1)}, bf16[256,512]{1,0:T(8,128)(2,1)S(1)}, u32[]{:S(2)}, u32[]{:S(2)}) collective-permute-start(bf16[256,512]{1,0:T(8,128)(2,1)S(1)} %get-tuple-element.38), channel_id=1, source_target_pairs={{0,3},{1,2},{2,1},{3,0},{4,7},{5,6},{6,5},{7,4},{8,11},{9,10},{10,... | collective-permute-start | bytes 786440 | tf_op jit(solution)/shard_map/ppermute | solution.py:213
  16.9 12.0 %collective-permute-start.4 = (bf16[816,128]{1,0:T(8,128)(2,1)S(1)}, bf16[816,128]{1,0:T(8,128)(2,1)S(1)}, u32[]{:S(2)}, u32[]{:S(2)}) collective-permute-start(bf16[816,128]{1,0:T(8,128)(2,1)S(1)} %get-tuple-element.34), channel_id=1, source_target_pairs={{0,8},{1,9},{2,10},{3,11},{4,12},{5,13},{6,14},{7,15},{8,16},{9,17... | collective-permute-start | bytes 626696 | tf_op jit(solution)/shard_map/ppermute | solution.py:216
  44.3 12.9 %collective-permute-start.11 = (bf16[1024,128]{1,0:T(8,128)(2,1)S(1)}, bf16[1024,128]{1,0:T(8,128)(2,1)S(1)}, u32[]{:S(2)}, u32[]{:S(2)}) collective-permute-start(bf16[1024,128]{1,0:T(8,128)(2,1)S(1)} %get-tuple-element.46), channel_id=1, source_target_pairs={{0,28},{1,29},{2,30},{3,31},{4,0},{5,1},{6,2},{7,3},{8,4},{9,5},{1... | collective-permute-start | bytes 786440 | tf_op jit(solution)/shard_map/ppermute | solution.py:216
  47.2 12.9 %collective-permute-start.8 = (bf16[256,512]{1,0:T(8,128)(2,1)S(1)}, bf16[256,512]{1,0:T(8,128)(2,1)S(1)}, u32[]{:S(2)}, u32[]{:S(2)}) collective-permute-start(bf16[256,512]{1,0:T(8,128)(2,1)S(1)} %get-tuple-element.40), channel_id=1, source_target_pairs={{0,1},{1,0},{2,3},{3,2},{4,5},{5,4},{6,7},{7,6},{8,9},{9,8},{10,11... | collective-permute-start | bytes 786440 | tf_op jit(solution)/shard_map/ppermute | solution.py:213
  47.7 9.5 %collective-permute-start.12 = (bf16[768,128]{1,0:T(8,128)(2,1)S(1)}, bf16[768,128]{1,0:T(8,128)(2,1)S(1)}, u32[]{:S(2)}, u32[]{:S(2)}) collective-permute-start(bf16[768,128]{1,0:T(8,128)(2,1)S(1)} %get-tuple-element.47), channel_id=1, source_target_pairs={{0,24},{1,25},{2,26},{3,27},{4,28},{5,29},{6,30},{7,31},{8,0},{9,1... | collective-permute-start | bytes 589832 | tf_op jit(solution)/shard_map/ppermute | solution.py:216
  49.3 11.4 %collective-permute-start.9 = (bf16[256,512]{1,0:T(8,128)(2,1)S(1)}, bf16[256,512]{1,0:T(8,128)(2,1)S(1)}, u32[]{:S(2)}, u32[]{:S(2)}) collective-permute-start(bf16[256,512]{1,0:T(8,128)(2,1)S(1)} %get-tuple-element.41), channel_id=1, source_target_pairs={{0,2},{1,3},{2,0},{3,1},{4,6},{5,7},{6,4},{7,5},{8,10},{9,11},{10,... | collective-permute-start | bytes 786440 | tf_op jit(solution)/shard_map/ppermute | solution.py:213
  50.4 13.3 %collective-permute-start.10 = (bf16[256,512]{1,0:T(8,128)(2,1)S(1)}, bf16[256,512]{1,0:T(8,128)(2,1)S(1)}, u32[]{:S(2)}, u32[]{:S(2)}) collective-permute-start(bf16[256,512]{1,0:T(8,128)(2,1)S(1)} %get-tuple-element.42), channel_id=1, source_target_pairs={{0,3},{1,2},{2,1},{3,0},{4,7},{5,6},{6,5},{7,4},{8,11},{9,10},{10,... | collective-permute-start | bytes 786440 | tf_op jit(solution)/shard_map/ppermute | solution.py:213
  57.9 7.4 %collective-permute-start.13 = (bf16[256,128]{1,0:T(8,128)(2,1)S(1)}, bf16[256,128]{1,0:T(8,128)(2,1)S(1)}, u32[]{:S(2)}, u32[]{:S(2)}) collective-permute-start(bf16[256,128]{1,0:T(8,128)(2,1)S(1)} %get-tuple-element.49), channel_id=1, source_target_pairs={{0,1},{1,0},{2,3},{3,2},{4,5},{5,4},{6,7},{7,6},{8,9},{9,8},{10,11... | collective-permute-start | bytes 196616 | tf_op jit(solution)/shard_map/ppermute | solution.py:213
  59.0 6.3 %collective-permute-start.14 = (bf16[256,128]{1,0:T(8,128)(2,1)S(1)}, bf16[256,128]{1,0:T(8,128)(2,1)S(1)}, u32[]{:S(2)}, u32[]{:S(2)}) collective-permute-start(bf16[256,128]{1,0:T(8,128)(2,1)S(1)} %get-tuple-element.50), channel_id=1, source_target_pairs={{0,2},{1,3},{2,0},{3,1},{4,6},{5,7},{6,4},{7,5},{8,10},{9,11},{10,... | collective-permute-start | bytes 196616 | tf_op jit(solution)/shard_map/ppermute | solution.py:213
  60.0 5.7 %collective-permute-start.15 = (bf16[256,128]{1,0:T(8,128)(2,1)S(1)}, bf16[256,128]{1,0:T(8,128)(2,1)S(1)}, u32[]{:S(2)}, u32[]{:S(2)}) collective-permute-start(bf16[256,128]{1,0:T(8,128)(2,1)S(1)} %get-tuple-element.51), channel_id=1, source_target_pairs={{0,3},{1,2},{2,1},{3,0},{4,7},{5,6},{6,5},{7,4},{8,11},{9,10},{10,... | collective-permute-start | bytes 196616 | tf_op jit(solution)/shard_map/ppermute | solution.py:213

commit v2 on v1

v2 whole, which is shorter than its diff:
```python
import functools
import math

import jax
import jax.numpy as jnp
from jax import lax
from jax.experimental import pallas as pl
from jax.experimental.pallas import tpu as pltpu
from jax.sharding import PartitionSpec as P

HEADS = 16
KV_HEADS = 4
HEAD = 128
WINDOW = 8
AXES = ("dp", "group")
GROUPS = HEADS // KV_HEADS
EXTRA = 16

VMEM = pl.BlockSpec(memory_space=pltpu.VMEM)
SMEM = pl.BlockSpec(memory_space=pltpu.SMEM)
ANY = pl.BlockSpec(memory_space=pl.ANY)
BF16 = jnp.bfloat16
F32 = jnp.float32


def rows_at(index, rows):
    return pl.ds(pl.multiple_of(index * rows, rows), rows)


def call(kernel, name, outs, operands, scratch=(), in_space=VMEM, out_space=VMEM):
    return pl.pallas_call(
        kernel,
        out_shape=[jax.ShapeDtypeStruct(shape, dtype) for shape, dtype in outs],
        in_specs=[SMEM] + [in_space] * (len(operands) - 1),
        out_specs=[out_space] * len(outs),
        scratch_shapes=list(scratch),
        compiler_params=pltpu.CompilerParams(vmem_limit_bytes=48 * 1024 * 1024),
        name=name,
    )(*operands)


def in_hbm(value):
    return pltpu.with_memory_space_constraint(value, pltpu.HBM)


def copy_all(pairs, sems):
    copies = [pltpu.make_async_copy(a, b, sems.at[i]) for i, (a, b) in enumerate(pairs)]
    for copy in copies:
        copy.start()
    return copies


def wait_all(copies):
    for copy in copies:
        copy.wait()


def pack_keys(tok, info, ids, keys, values, s0, s1, s2, s3, ids_here, sems):
    me = info[0]
    slots = (s0, s1, s2, s3)
    pairs = [(ids, ids_here)]
    for s, slot in enumerate(slots):
        columns = rows_at(me ^ s, HEAD)
        pairs.append((keys.at[:, columns], slot.at[0:tok, :]))
        pairs.append((values.at[:, columns], slot.at[tok : 2 * tok, :]))
    copies = copy_all(pairs, sems)
    copies[0].wait()
    along = jnp.broadcast_to(ids_here[...], (tok, tok)).astype(F32)
    down = along.T
    local_start = jnp.sum((down < along).astype(F32), axis=0, keepdims=True)
    low = (ids_here[...] & 255).astype(F32)
    high = (ids_here[...] >> 8).astype(F32)
    marks = jnp.concatenate(
        [local_start, low, high, jnp.zeros((EXTRA - 3, tok), F32)], 0
    ).astype(BF16)
    for slot in slots:
        slot[2 * tok : 2 * tok + EXTRA, :] = marks
    wait_all(copies[1:])


def pack_queries(tok, info, queries, grads, s0, s1, s2, s3, sems):
    me = info[0]
    pairs = []
    for s, slot in enumerate((s0, s1, s2, s3)):
        columns = rows_at(me ^ s, GROUPS * HEAD)
        pairs.append((queries.at[:, columns], slot.at[0:tok, :]))
        pairs.append((grads.at[:, columns], slot.at[tok : 2 * tok, :]))
    copies = copy_all(pairs, sems)
    for slot in (s1, s2, s3):
        slot[2 * tok :, :] = jnp.zeros((slot.shape[0] - 2 * tok, slot.shape[1]), BF16)
    wait_all(copies)


def order_keys(tok, info, s0, s1, s2, s3, near, far, marks):
    me = info[0]
    n = KV_HEADS
    marks[...] = jnp.zeros_like(marks)
    for s, slot in enumerate((s0, s1, s2, s3)):
        block = me ^ s
        near[rows_at(block, tok), :] = slot[0:tok, :]
        near[rows_at(n + block, tok), :] = slot[tok : 2 * tok, :]
        mark = slot[2 * tok : 2 * tok + EXTRA, :].astype(F32)
        for kind in range(3):
            marks[pl.ds(kind * n + block, 1), :] = mark[kind : kind + 1]
    near[2 * n * tok :, :] = marks[...].astype(BF16)
    far[0 : 3 * tok, :] = near[tok : n * tok, :]
    far[3 * tok : 6 * tok, :] = near[(n + 1) * tok : 2 * n * tok, :]
    far[6 * tok :, :] = near[2 * n * tok :, :]


def attend(
    tok, info, own, near, far, q0, q1, q2, q3,
    r0, r1, r2, r3, own_terms, near_terms, far_terms,
    key_rows, value_rows, key_cols, value_cols, marks, grad_keys, grad_values,
):
    me, quad = info[0], info[1]
    n = KV_HEADS
    span = WINDOW * tok
    before = span - tok
    blocks = 3 * n - 1
    key_rows[0 : 3 * tok, :] = far[0 : 3 * tok, :]
    key_rows[3 * tok : 7 * tok, :] = near[0 : 4 * tok, :]
    key_rows[7 * tok :, :] = own[0 : 4 * tok, :]
    value_rows[0 : 3 * tok, :] = far[3 * tok : 6 * tok, :]
    value_rows[3 * tok : 7 * tok, :] = near[4 * tok : 8 * tok, :]
    value_rows[7 * tok :, :] = own[4 * tok : 8 * tok, :]
    for b in range(blocks):
        at = slice(b * tok, (b + 1) * tok)
        key_cols[:, at] = key_rows[at, :].T
        value_cols[:, at] = value_rows[at, :].T
    for first, count, source in ((0, 3, far), (3, 4, near), (7, 4, own)):
        mark = source[source.shape[0] - EXTRA :, :].astype(F32)
        ids = mark[n : 2 * n] + 256.0 * mark[2 * n : 3 * n]
        exists = (quad - 2) * n + first + 1 >= 0
        marks[first : first + count, :] = jnp.where(exists, ids[n - count : n], -1.0)
        if source is own:
            marks[16 : 16 + n, :] = mark[0:n]
    marks[blocks:16, :] = jnp.full((16 - blocks, tok), -1.0, F32)
    grad_keys[...] = jnp.zeros_like(grad_keys)
    grad_values[...] = jnp.zeros_like(grad_values)
    scale = HEAD ** (-0.5)
    key_place = lax.broadcasted_iota(jnp.int32, (span, tok), 0)
    query_limit = before + lax.broadcasted_iota(jnp.int32, (1, tok), 1)
    mark_row = lax.broadcasted_iota(jnp.int32, (16, tok), 0)

    for s, (piece, result) in enumerate(((q0, r0), (q1, r1), (q2, r2), (q3, r3))):
        block = me ^ s
        window = pl.ds(pl.multiple_of(block * tok, tok), span)
        all_ids = marks[0:16, :]
        first = jnp.min(marks[pl.ds(block + 7, 1), :], axis=1, keepdims=True)
        earlier = (mark_row >= block) & (mark_row < block + 7) & (all_ids < first)
        count = jnp.sum(
            jnp.sum(earlier.astype(F32), axis=1, keepdims=True), axis=0, keepdims=True
        )
        local_start = marks[pl.ds(16 + block, 1), :]
        start = jnp.where(local_start == 0.0, count, before + local_start).astype(jnp.int32)
        allowed = (key_place >= start) & (key_place <= query_limit)
        bias = jnp.where(allowed, 0.0, -jnp.inf)
        bias = jnp.concatenate([bias] * GROUPS, 1)
        query = jnp.concatenate(
            [piece[0:tok, h * HEAD : (h + 1) * HEAD] for h in range(GROUPS)], 0
        )
        grad = jnp.concatenate(
            [piece[tok : 2 * tok, h * HEAD : (h + 1) * HEAD] for h in range(GROUPS)], 0
        )
        scores = lax.dot_general(
            key_rows[window, :], query, (((1,), (1,)), ((), ())), preferred_element_type=F32
        )
        scores = scores + bias
        top = jnp.max(scores, axis=0, keepdims=True)
        weights = jnp.exp2((scores - top) * (scale * math.log2(math.e)))
        total = jnp.sum(weights, axis=0, keepdims=True)
        probs = weights * (1.0 / total)
        probs_low = probs.astype(BF16)
        output = jnp.dot(value_cols[:, window], probs_low, preferred_element_type=F32)
        output = output.astype(BF16).astype(F32)
        grad_probs = lax.dot_general(
            value_rows[window, :], grad, (((1,), (1,)), ((), ())), preferred_element_type=F32
        )
        grad_cols = jnp.concatenate(
            [grad[h * tok : (h + 1) * tok].T for h in range(GROUPS)], 1
        ).astype(F32)
        delta = jnp.sum(grad_cols * output, axis=0, keepdims=True)
        grad_scores = (probs * (grad_probs - delta)).astype(BF16)
        grad_query = jnp.dot(key_cols[:, window], grad_scores, preferred_element_type=F32)
        grad_query = grad_query * scale
        grad_values[window, :] += jnp.dot(probs_low, grad, preferred_element_type=F32)
        grad_keys[window, :] += jnp.dot(grad_scores, query, preferred_element_type=F32)
        for h in range(GROUPS):
            part = slice(h * tok, (h + 1) * tok)
            columns = slice(h * HEAD, (h + 1) * HEAD)
            result[0:tok, columns] = output[:, part].T.astype(BF16)
            result[tok : 2 * tok, columns] = grad_query[:, part].T.astype(BF16)

    far_terms[0 : 3 * tok, :] = (grad_keys[0 : 3 * tok, :] * scale).astype(BF16)
    far_terms[3 * tok :, :] = grad_values[0 : 3 * tok, :].astype(BF16)
    near_terms[0 : 4 * tok, :] = (grad_keys[3 * tok : 7 * tok, :] * scale).astype(BF16)
    near_terms[4 * tok :, :] = grad_values[3 * tok : 7 * tok, :].astype(BF16)
    own_terms[0 : 4 * tok, :] = grad_keys[7 * tok :, :] * scale
    own_terms[4 * tok :, :] = grad_values[7 * tok :, :]


def add_terms(tok, info, own, near, far, s0, s1, s2, s3, total):
    me = info[0]
    n = KV_HEADS
    total[...] = own[...] + near[...].astype(F32)
    total[tok : n * tok, :] += far[0 : 3 * tok, :].astype(F32)
    total[(n + 1) * tok :, :] += far[3 * tok :, :].astype(F32)
    for s, slot in enumerate((s0, s1, s2, s3)):
        slot[0:tok, :] = total[rows_at(me ^ s, tok), :].astype(BF16)
        slot[tok : 2 * tok, :] = total[rows_at(n + (me ^ s), tok), :].astype(BF16)


def place_columns(tok, width, info, s0, s1, s2, s3, upper, lower, sems):
    me = info[0]
    pairs = []
    for s, slot in enumerate((s0, s1, s2, s3)):
        columns = rows_at(me ^ s, width)
        pairs.append((slot.at[0:tok], upper.at[:, columns]))
        pairs.append((slot.at[tok : 2 * tok], lower.at[:, columns]))
    wait_all(copy_all(pairs, sems))


def local(queries, key_states, value_states, grad_out, doc_ids):
    tok = queries.shape[0]
    n = KV_HEADS
    count = lax.axis_size("dp") * lax.axis_size("group")
    rank = lax.axis_index(AXES)
    info = jnp.stack([rank % n, rank // n]).astype(jnp.int32)

    def swap(value, bits):
        return lax.ppermute(value, AXES, [(i, i ^ bits) for i in range(count)])

    def ring(value, steps):
        return lax.ppermute(value, AXES, [(i, (i + steps) % count) for i in range(count)])

    def exchange(slots):
        return [slots[0]] + [swap(slots[s], s) for s in range(1, n)]

    dma = pltpu.SemaphoreType.DMA
    kv_slots = call(
        functools.partial(pack_keys, tok),
        "pack_keys",
        [((2 * tok + EXTRA, HEAD), BF16)] * n,
        (info, in_hbm(doc_ids[None, :]), in_hbm(key_states), in_hbm(value_states)),
        [pltpu.VMEM((1, tok), jnp.int32), dma((9,))],
        in_space=ANY,
    )
    kv_slots = exchange(kv_slots)
    query_slots = call(
        functools.partial(pack_queries, tok),
        "pack_queries",
        [((2 * tok + EXTRA, GROUPS * HEAD), BF16)] * n,
        (info, in_hbm(queries), in_hbm(grad_out)),
        [dma((8,))],
        in_space=ANY,
    )
    query_slots = exchange(query_slots)
    own, own_late = call(
        functools.partial(order_keys, tok),
        "order_keys",
        [((2 * n * tok + EXTRA, HEAD), BF16), ((6 * tok + EXTRA, HEAD), BF16)],
        (info, *kv_slots),
        [pltpu.VMEM((EXTRA, HEAD), F32)],
    )
    near = ring(own, n)
    far = ring(own_late, 2 * n)
    blocks = 3 * n - 1
    results = call(
        functools.partial(attend, tok),
        "attend",
        [((2 * tok, GROUPS * HEAD), BF16)] * n
        + [((2 * n * tok, HEAD), F32), ((2 * n * tok, HEAD), BF16), ((6 * tok, HEAD), BF16)],
        (info, own, near, far, *query_slots),
        [
            pltpu.VMEM((blocks * tok, HEAD), BF16),
            pltpu.VMEM((blocks * tok, HEAD), BF16),
            pltpu.VMEM((HEAD, blocks * tok), BF16),
            pltpu.VMEM((HEAD, blocks * tok), BF16),
            pltpu.VMEM((24, tok), F32),
            pltpu.VMEM((blocks * tok, HEAD), F32),
            pltpu.VMEM((blocks * tok, HEAD), F32),
        ],
    )
    out_slots, (own_terms, near_terms, far_terms) = results[:n], results[n:]
    near_back = ring(near_terms, -n)
    far_back = ring(far_terms, -2 * n)
    out_slots = exchange(out_slots)
    grad_slots = call(
        functools.partial(add_terms, tok),
        "add_terms",
        [((2 * tok, HEAD), BF16)] * n,
        (info, own_terms, near_back, far_back),
        [pltpu.VMEM((2 * n * tok, HEAD), F32)],
    )
    grad_slots = exchange(grad_slots)
    attended, grad_queries = call(
        functools.partial(place_columns, tok, GROUPS * HEAD),
        "place_queries",
        [((tok, HEADS * HEAD), BF16)] * 2,
        (info, *out_slots),
        [dma((8,))],
        out_space=ANY,
    )
    grad_keys, grad_values = call(
        functools.partial(place_columns, tok, HEAD),
        "place_keys",
        [((tok, KV_HEADS * HEAD), BF16)] * 2,
        (info, *grad_slots),
        [dma((8,))],
        out_space=ANY,
    )
    return (attended, grad_queries, grad_keys, grad_values)


def solution(mesh):
    rows = P(AXES, None)
    return jax.shard_map(
        local,
        mesh=mesh,
        in_specs=(rows, rows, rows, rows, P(AXES)),
        out_specs=(rows, rows, rows, rows),
        check_vma=False,
    )
```

time: 67.3 us -> 55.3 us (0.82)
  waiting for transfers between devices: 24.2 us -> 18 us
  Pallas kernels: 20.8 us -> 16.4 us
  local copies, waits for them, and re-layouts: 3.56 us -> 0 us
  starting transfers between devices: 17.7 us -> 19.6 us
    ppermute x12, waiting for transfers between devices: 18.2 us -> 3.93 us  [swap(): return lax.ppermute(value, AXES, [(i, i ^ bits) for i in range(count)])]
    ppermute x4, waiting for transfers between devices: 5.97 us -> 14 us  [ring(): lax.ppermute(value, AXES, [(i, (i + steps) % count) for i in range(count)])]
    pallas_call x7, Pallas kernels: 20.8 us -> 16.4 us  [call(): pl.pallas_call(kernel, out_shape=[jax.ShapeDtypeStruct(shape, dtype) for...]
    unnamed x10 -> x0, local copies, waits for them, and re-layouts: 3.56 us -> none
    ppermute x4, starting transfers between devices: 7.14 us -> 8.37 us  [ring(): lax.ppermute(value, AXES, [(i, (i + steps) % count) for i in range(count)])]
    ppermute x12, starting transfers between devices: 10.5 us -> 11.3 us  [swap(): return lax.ppermute(value, AXES, [(i, i ^ bits) for i in range(count)])]
  transfers between devices with their start and end apart: 16 -> 16, of which waited for: 7 -> 5; matrix products, arithmetic and copies ran while one was open for 0% -> 0% of each run, Pallas kernels for 4% -> 9%
where the time goes in v2:
time: 55.3 us; the launch traced here: 54.8 us
  starting transfers between devices  19.6 us (35%)
  waiting for transfers between devices  18 us (33%)
  Pallas kernels  16.4 us (30%)
  between operations  0.73 us (1%)
    pallas_call x7, Pallas kernels, call(): pl.pallas_call(kernel, out_shape=[jax.ShapeDtypeStruct(shape, dtype) for...  16.4 us
    ppermute x4, waiting for transfers between devices, ring(): lax.ppermute(value, AXES, [(i, (i + steps) % count) for i in range(count)])  14 us
    ppermute x12, starting transfers between devices, swap(): return lax.ppermute(value, AXES, [(i, i ^ bits) for i in range(count)])  11.3 us
    ppermute x4, starting transfers between devices, ring(): lax.ppermute(value, AXES, [(i, (i + steps) % count) for i in range(count)])  8.37 us
    ppermute x12, waiting for transfers between devices, swap(): return lax.ppermute(value, AXES, [(i, i ^ bits) for i in range(count)])  3.93 us
  transfers between devices with their start and end apart: 16, of which 5 were waited for; matrix products, arithmetic and copies ran while one was open for 0% of the time, Pallas kernels for 9%

profile of v2, /device:TPU:1, one launch (start us, length us, event | category | flops | bytes accessed | tf_op | source)
XLA Modules:
  0.0 54.8 jit_solution(17455382054870926412)
XLA Ops:
  0.7 0.1 pad_add_fusion.info
  0.7 1.5 %pack_keys.1 = (bf16[272,128]{1,0:T(8,128)(2,1)S(1)}, bf16[272,128]{1,0:T(8,128)(2,1)S(1)}, bf16[272,128]{1,0:T(8,128)(2,1)S(1)}, bf16[272,128]{1,0:T(8,128)(2,1)S(1)}) custom-call(s32[2]{0:T(128)S(1)} %pad_add_fusion.info, s32[1,128]{1,0:T(1,128)} %bitcast.3, bf16[128,512]{1,0:T(8,128)(2,1)} %keys.1, bf16[128,512]{1,0:T(8,128)(2,1)} %values.1), custom_call_target="tpu_custom_call" | custom-call | tf_op jit(solution)/shard_map/pack_keys/pallas_call | solution.py:31
  2.2 0.1 collective-permute-start
  2.4 2.7 %collective-permute-start.1 = (bf16[272,128]{1,0:T(8,128)(2,1)S(1)}, bf16[272,128]{1,0:T(8,128)(2,1)S(1)}, u32[]{:S(2)}, u32[]{:S(2)}) collective-permute-start(bf16[272,128]{1,0:T(8,128)(2,1)S(1)} %get-tuple-element.31), channel_id=1, source_target_pairs={{0,2},{1,3},{2,0},{3,1},{4,6},{5,7},{6,4},{7,5},{8,10},{9,11},{10,... | collective-permute-start | bytes 208904 | tf_op jit(solution)/shard_map/ppermute | solution.py:232
  5.0 0.0 collective-permute-start.2
  5.1 1.9 %pack_queries.1 = (bf16[272,512]{1,0:T(8,128)(2,1)S(1)}, bf16[272,512]{1,0:T(8,128)(2,1)S(1)}, bf16[272,512]{1,0:T(8,128)(2,1)S(1)}, bf16[272,512]{1,0:T(8,128)(2,1)S(1)}) custom-call(s32[2]{0:T(128)S(1)} %pad_add_fusion.info, bf16[128,2048]{1,0:T(8,128)(2,1)} %queries.1, bf16[128,2048]{1,0:T(8,128)(2,1)} %grads.1), custom_call_target="tpu_custom_call" | custom-call | tf_op jit(solution)/shard_map/pack_queries/pallas_call | solution.py:31
  7.0 0.4 collective-permute-start.5
  7.4 1.4 %collective-permute-start.6 = (bf16[272,512]{1,0:T(8,128)(2,1)S(1)}, bf16[272,512]{1,0:T(8,128)(2,1)S(1)}, u32[]{:S(2)}, u32[]{:S(2)}) collective-permute-start(bf16[272,512]{1,0:T(8,128)(2,1)S(1)} %get-tuple-element.37), channel_id=1, source_target_pairs={{0,2},{1,3},{2,0},{3,1},{4,6},{5,7},{6,4},{7,5},{8,10},{9,11},{10,... | collective-permute-start | bytes 835592 | tf_op jit(solution)/shard_map/ppermute | solution.py:232
  8.9 0.0 collective-permute-done.s1
  8.9 0.3 collective-permute-start.7
  9.2 0.6 %order_keys.1 = (bf16[1040,128]{1,0:T(8,128)(2,1)S(1)}, bf16[784,128]{1,0:T(8,128)(2,1)S(1)}) custom-call(s32[2]{0:T(128)S(1)} %pad_add_fusion.info, bf16[272,128]{1,0:T(8,128)(2,1)S(1)} %get-tuple-element.29.s0, bf16[272,128]{1,0:T(8,128)(2,1)S(1)} %collective-permute-done.s1, bf16[272,128]{1,0:T(8,128)(2,1)S(1)} %collective-permute-done.1.s2, ...), custom_call_target="tpu_custom_call" | custom-call | tf_op jit(solution)/shard_map/order_keys/pallas_call | solution.py:31
  9.8 1.7 %collective-permute-start.3 = (bf16[1040,128]{1,0:T(8,128)(2,1)S(1)}, bf16[1040,128]{1,0:T(8,128)(2,1)S(1)}, u32[]{:S(2)}, u32[]{:S(2)}) collective-permute-start(bf16[1040,128]{1,0:T(8,128)(2,1)S(1)} %get-tuple-element.33.own), channel_id=1, source_target_pairs={{0,4},{1,5},{2,6},{3,7},{4,8},{5,9},{6,10},{7,11},{8,12},{9,13},{1... | collective-permute-start | bytes 798728 | tf_op jit(solution)/shard_map/ppermute | solution.py:235
  11.5 1.3 %collective-permute-start.4 = (bf16[784,128]{1,0:T(8,128)(2,1)S(1)}, bf16[784,128]{1,0:T(8,128)(2,1)S(1)}, u32[]{:S(2)}, u32[]{:S(2)}) collective-permute-start(bf16[784,128]{1,0:T(8,128)(2,1)S(1)} %get-tuple-element.34), channel_id=1, source_target_pairs={{0,8},{1,9},{2,10},{3,11},{4,12},{5,13},{6,14},{7,15},{8,16},{9,17... | collective-permute-start | bytes 602120 | tf_op jit(solution)/shard_map/ppermute | solution.py:235
  12.8 7.0 %collective-permute-done.4.far = bf16[784,128]{1,0:T(8,128)(2,1)S(1)} collective-permute-done((bf16[784,128]{1,0:T(8,128)(2,1)S(1)}, bf16[784,128]{1,0:T(8,128)(2,1)S(1)}, u32[]{:S(2)}, u32[]{:S(2)}) %collective-permute-start.4) | collective-permute-done | bytes 200736 | tf_op jit(solution)/shard_map/ppermute | solution.py:235
  19.8 0.0 collective-permute-done.5.q1
  19.8 2.0 %collective-permute-done.7.q3 = bf16[272,512]{1,0:T(8,128)(2,1)S(1)} collective-permute-done((bf16[272,512]{1,0:T(8,128)(2,1)S(1)}, bf16[272,512]{1,0:T(8,128)(2,1)S(1)}, u32[]{:S(2)}, u32[]{:S(2)}) %collective-permute-start.7) | collective-permute-done | bytes 278560 | tf_op jit(solution)/shard_map/ppermute | solution.py:232
  21.8 0.0 collective-permute-done.3.near
  21.8 8.9 %attend.1 = (bf16[256,512]{1,0:T(8,128)(2,1)S(1)}, bf16[256,512]{1,0:T(8,128)(2,1)S(1)}, bf16[256,512]{1,0:T(8,128)(2,1)S(1)}, bf16[256,512]{1,0:T(8,128)(2,1)S(...) custom-call(s32[2]{0:T(128)S(1)} %pad_add_fusion.info, ...), custom_call_target="tpu_custom_call" | custom-call | tf_op jit(solution)/shard_map/attend/pallas_call | solution.py:31
  30.6 5.2 %collective-permute-start.11 = (bf16[1024,128]{1,0:T(8,128)(2,1)S(1)}, bf16[1024,128]{1,0:T(8,128)(2,1)S(1)}, u32[]{:S(2)}, u32[]{:S(2)}) collective-permute-start(bf16[1024,128]{1,0:T(8,128)(2,1)S(1)} %get-tuple-element.46), channel_id=1, source_target_pairs={{0,28},{1,29},{2,30},{3,31},{4,0},{5,1},{6,2},{7,3},{8,4},{9,5},{1... | collective-permute-start | bytes 786440 | tf_op jit(solution)/shard_map/ppermute | solution.py:235
  35.8 1.0 %collective-permute-start.8 = (bf16[256,512]{1,0:T(8,128)(2,1)S(1)}, bf16[256,512]{1,0:T(8,128)(2,1)S(1)}, u32[]{:S(2)}, u32[]{:S(2)}) collective-permute-start(bf16[256,512]{1,0:T(8,128)(2,1)S(1)} %get-tuple-element.40), channel_id=1, source_target_pairs={{0,1},{1,0},{2,3},{3,2},{4,5},{5,4},{6,7},{7,6},{8,9},{9,8},{10,11... | collective-permute-start | bytes 786440 | tf_op jit(solution)/shard_map/ppermute | solution.py:232
  36.9 0.2 collective-permute-start.12
  37.0 1.2 %collective-permute-start.9 = (bf16[256,512]{1,0:T(8,128)(2,1)S(1)}, bf16[256,512]{1,0:T(8,128)(2,1)S(1)}, u32[]{:S(2)}, u32[]{:S(2)}) collective-permute-start(bf16[256,512]{1,0:T(8,128)(2,1)S(1)} %get-tuple-element.41), channel_id=1, source_target_pairs={{0,2},{1,3},{2,0},{3,1},{4,6},{5,7},{6,4},{7,5},{8,10},{9,11},{10,... | collective-permute-start | bytes 786440 | tf_op jit(solution)/shard_map/ppermute | solution.py:232
  38.2 0.7 %collective-permute-start.10 = (bf16[256,512]{1,0:T(8,128)(2,1)S(1)}, bf16[256,512]{1,0:T(8,128)(2,1)S(1)}, u32[]{:S(2)}, u32[]{:S(2)}) collective-permute-start(bf16[256,512]{1,0:T(8,128)(2,1)S(1)} %get-tuple-element.42), channel_id=1, source_target_pairs={{0,3},{1,2},{2,1},{3,0},{4,7},{5,6},{6,5},{7,4},{8,11},{9,10},{10,... | collective-permute-start | bytes 786440 | tf_op jit(solution)/shard_map/ppermute | solution.py:232
  38.9 7.1 %collective-permute-done.12.far = bf16[768,128]{1,0:T(8,128)(2,1)S(1)} collective-permute-done((bf16[768,128]{1,0:T(8,128)(2,1)S(1)}, bf16[768,128]{1,0:T(8,128)(2,1)S(1)}, u32[]{:S(2)}, u32[]{:S(2)}) %collective-permute-start.12) | collective-permute-done | bytes 196640 | tf_op jit(solution)/shard_map/ppermute | solution.py:235
  46.0 0.7 %add_terms.1 = (bf16[256,128]{1,0:T(8,128)(2,1)S(1)}, bf16[256,128]{1,0:T(8,128)(2,1)S(1)}, bf16[256,128]{1,0:T(8,128)(2,1)S(1)}, bf16[256,128]{1,0:T(8,128)(2,1)S(1)}) custom-call(s32[2]{0:T(128)S(1)} %pad_add_fusion.info, f32[1024,128]{1,0:T(8,128)S(1)} %get-tuple-element.45.own, bf16[1024,128]{1,0:T(8,128)(2,1)S(1)} %collective-permute-done.11.near, ...), custom_call_target="tpu_custom_call" | custom-call | tf_op jit(solution)/shard_map/add_terms/pallas_call | solution.py:31
  46.7 1.6 %collective-permute-start.13 = (bf16[256,128]{1,0:T(8,128)(2,1)S(1)}, bf16[256,128]{1,0:T(8,128)(2,1)S(1)}, u32[]{:S(2)}, u32[]{:S(2)}) collective-permute-start(bf16[256,128]{1,0:T(8,128)(2,1)S(1)} %get-tuple-element.49), channel_id=1, source_target_pairs={{0,1},{1,0},{2,3},{3,2},{4,5},{5,4},{6,7},{7,6},{8,9},{9,8},{10,11... | collective-permute-start | bytes 196616 | tf_op jit(solution)/shard_map/ppermute | solution.py:232
  48.2 1.2 %collective-permute-start.14 = (bf16[256,128]{1,0:T(8,128)(2,1)S(1)}, bf16[256,128]{1,0:T(8,128)(2,1)S(1)}, u32[]{:S(2)}, u32[]{:S(2)}) collective-permute-start(bf16[256,128]{1,0:T(8,128)(2,1)S(1)} %get-tuple-element.50), channel_id=1, source_target_pairs={{0,2},{1,3},{2,0},{3,1},{4,6},{5,7},{6,4},{7,5},{8,10},{9,11},{10,... | collective-permute-start | bytes 196616 | tf_op jit(solution)/shard_map/ppermute | solution.py:232
  49.4 0.5 collective-permute-start.15
  49.9 0.7 %collective-permute-done.10.s3 = bf16[256,512]{1,0:T(8,128)(2,1)S(1)} collective-permute-done((bf16[256,512]{1,0:T(8,128)(2,1)S(1)}, bf16[256,512]{1,0:T(8,128)(2,1)S(1)}, u32[]{:S(2)}, u32[]{:S(2)}) %collective-permute-start.10) | collective-permute-done | bytes 262176 | tf_op jit(solution)/shard_map/ppermute | solution.py:232
  50.7 1.6 %place_queries.1 = (bf16[128,2048]{1,0:T(8,128)(2,1)}, bf16[128,2048]{1,0:T(8,128)(2,1)}) custom-call(s32[2]{0:T(128)S(1)} %pad_add_fusion.info, bf16[256,512]{1,0:T(8,128)(2,1)S(1)} %get-tuple-element.39.s0, bf16[256,512]{1,0:T(8,128)(2,1)S(1)} %collective-permute-done.8.s1, bf16[256,512]{1,0:T(8,128)(2,1)S(1)} %collective-permute-done.9.s2, ...), custom_call_target="tpu_custom_call" | custom-call | tf_op jit(solution)/shard_map/place_queries/pallas_call | solution.py:31
  52.3 1.2 %collective-permute-done.15.s3 = bf16[256,128]{1,0:T(8,128)(2,1)S(1)} collective-permute-done((bf16[256,128]{1,0:T(8,128)(2,1)S(1)}, bf16[256,128]{1,0:T(8,128)(2,1)S(1)}, u32[]{:S(2)}, u32[]{:S(2)}) %collective-permute-start.15) | collective-permute-done | bytes 65568 | tf_op jit(solution)/shard_map/ppermute | solution.py:232
  53.5 1.3 %place_keys.1 = (bf16[128,512]{1,0:T(8,128)(2,1)}, bf16[128,512]{1,0:T(8,128)(2,1)}) custom-call(s32[2]{0:T(128)S(1)} %pad_add_fusion.info, bf16[256,128]{1,0:T(8,128)(2,1)S(1)} %get-tuple-element.48.s0, bf16[256,128]{1,0:T(8,128)(2,1)S(1)} %collective-permute-done.13.s1, bf16[256,128]{1,0:T(8,128)(2,1)S(1)} %collective-permute-done.14.s2, ...), custom_call_target="tpu_custom_call" | custom-call | tf_op jit(solution)/shard_map/place_keys/pallas_call | solution.py:31
  (8 shorter events, 0.0 us)
Async XLA Ops:
  2.2 6.6 %collective-permute-start = (bf16[272,128]{1,0:T(8,128)(2,1)S(1)}, bf16[272,128]{1,0:T(8,128)(2,1)S(1)}, u32[]{:S(2)}, u32[]{:S(2)}) collective-permute-start(bf16[272,128]{1,0:T(8,128)(2,1)S(1)} %get-tuple-element.30), channel_id=1, source_target_pairs={{0,1},{1,0},{2,3},{3,2},{4,5},{5,4},{6,7},{7,6},{8,9},{9,8},{10,11... | collective-permute-start | bytes 208904 | tf_op jit(solution)/shard_map/ppermute | solution.py:232
  2.4 6.9 %collective-permute-start.1 = (bf16[272,128]{1,0:T(8,128)(2,1)S(1)}, bf16[272,128]{1,0:T(8,128)(2,1)S(1)}, u32[]{:S(2)}, u32[]{:S(2)}) collective-permute-start(bf16[272,128]{1,0:T(8,128)(2,1)S(1)} %get-tuple-element.31), channel_id=1, source_target_pairs={{0,2},{1,3},{2,0},{3,1},{4,6},{5,7},{6,4},{7,5},{8,10},{9,11},{10,... | collective-permute-start | bytes 208904 | tf_op jit(solution)/shard_map/ppermute | solution.py:232
  5.0 4.2 %collective-permute-start.2 = (bf16[272,128]{1,0:T(8,128)(2,1)S(1)}, bf16[272,128]{1,0:T(8,128)(2,1)S(1)}, u32[]{:S(2)}, u32[]{:S(2)}) collective-permute-start(bf16[272,128]{1,0:T(8,128)(2,1)S(1)} %get-tuple-element.32), channel_id=1, source_target_pairs={{0,3},{1,2},{2,1},{3,0},{4,7},{5,6},{6,5},{7,4},{8,11},{9,10},{10,... | collective-permute-start | bytes 208904 | tf_op jit(solution)/shard_map/ppermute | solution.py:232
  7.0 12.8 %collective-permute-start.5 = (bf16[272,512]{1,0:T(8,128)(2,1)S(1)}, bf16[272,512]{1,0:T(8,128)(2,1)S(1)}, u32[]{:S(2)}, u32[]{:S(2)}) collective-permute-start(bf16[272,512]{1,0:T(8,128)(2,1)S(1)} %get-tuple-element.36), channel_id=1, source_target_pairs={{0,1},{1,0},{2,3},{3,2},{4,5},{5,4},{6,7},{7,6},{8,9},{9,8},{10,11... | collective-permute-start | bytes 835592 | tf_op jit(solution)/shard_map/ppermute | solution.py:232
  7.4 12.4 %collective-permute-start.6 = (bf16[272,512]{1,0:T(8,128)(2,1)S(1)}, bf16[272,512]{1,0:T(8,128)(2,1)S(1)}, u32[]{:S(2)}, u32[]{:S(2)}) collective-permute-start(bf16[272,512]{1,0:T(8,128)(2,1)S(1)} %get-tuple-element.37), channel_id=1, source_target_pairs={{0,2},{1,3},{2,0},{3,1},{4,6},{5,7},{6,4},{7,5},{8,10},{9,11},{10,... | collective-permute-start | bytes 835592 | tf_op jit(solution)/shard_map/ppermute | solution.py:232
  8.9 12.9 %collective-permute-start.7 = (bf16[272,512]{1,0:T(8,128)(2,1)S(1)}, bf16[272,512]{1,0:T(8,128)(2,1)S(1)}, u32[]{:S(2)}, u32[]{:S(2)}) collective-permute-start(bf16[272,512]{1,0:T(8,128)(2,1)S(1)} %get-tuple-element.38), channel_id=1, source_target_pairs={{0,3},{1,2},{2,1},{3,0},{4,7},{5,6},{6,5},{7,4},{8,11},{9,10},{10,... | collective-permute-start | bytes 835592 | tf_op jit(solution)/shard_map/ppermute | solution.py:232
  9.8 12.0 %collective-permute-start.3 = (bf16[1040,128]{1,0:T(8,128)(2,1)S(1)}, bf16[1040,128]{1,0:T(8,128)(2,1)S(1)}, u32[]{:S(2)}, u32[]{:S(2)}) collective-permute-start(bf16[1040,128]{1,0:T(8,128)(2,1)S(1)} %get-tuple-element.33.own), channel_id=1, source_target_pairs={{0,4},{1,5},{2,6},{3,7},{4,8},{5,9},{6,10},{7,11},{8,12},{9,13},{1... | collective-permute-start | bytes 798728 | tf_op jit(solution)/shard_map/ppermute | solution.py:235
  11.5 8.3 %collective-permute-start.4 = (bf16[784,128]{1,0:T(8,128)(2,1)S(1)}, bf16[784,128]{1,0:T(8,128)(2,1)S(1)}, u32[]{:S(2)}, u32[]{:S(2)}) collective-permute-start(bf16[784,128]{1,0:T(8,128)(2,1)S(1)} %get-tuple-element.34), channel_id=1, source_target_pairs={{0,8},{1,9},{2,10},{3,11},{4,12},{5,13},{6,14},{7,15},{8,16},{9,17... | collective-permute-start | bytes 602120 | tf_op jit(solution)/shard_map/ppermute | solution.py:235
  30.6 15.4 %collective-permute-start.11 = (bf16[1024,128]{1,0:T(8,128)(2,1)S(1)}, bf16[1024,128]{1,0:T(8,128)(2,1)S(1)}, u32[]{:S(2)}, u32[]{:S(2)}) collective-permute-start(bf16[1024,128]{1,0:T(8,128)(2,1)S(1)} %get-tuple-element.46), channel_id=1, source_target_pairs={{0,28},{1,29},{2,30},{3,31},{4,0},{5,1},{6,2},{7,3},{8,4},{9,5},{1... | collective-permute-start | bytes 786440 | tf_op jit(solution)/shard_map/ppermute | solution.py:235
  35.8 13.6 %collective-permute-start.8 = (bf16[256,512]{1,0:T(8,128)(2,1)S(1)}, bf16[256,512]{1,0:T(8,128)(2,1)S(1)}, u32[]{:S(2)}, u32[]{:S(2)}) collective-permute-start(bf16[256,512]{1,0:T(8,128)(2,1)S(1)} %get-tuple-element.40), channel_id=1, source_target_pairs={{0,1},{1,0},{2,3},{3,2},{4,5},{5,4},{6,7},{7,6},{8,9},{9,8},{10,11... | collective-permute-start | bytes 786440 | tf_op jit(solution)/shard_map/ppermute | solution.py:232
  36.9 9.2 %collective-permute-start.12 = (bf16[768,128]{1,0:T(8,128)(2,1)S(1)}, bf16[768,128]{1,0:T(8,128)(2,1)S(1)}, u32[]{:S(2)}, u32[]{:S(2)}) collective-permute-start(bf16[768,128]{1,0:T(8,128)(2,1)S(1)} %get-tuple-element.47), channel_id=1, source_target_pairs={{0,24},{1,25},{2,26},{3,27},{4,28},{5,29},{6,30},{7,31},{8,0},{9,1... | collective-permute-start | bytes 589832 | tf_op jit(solution)/shard_map/ppermute | solution.py:235
  37.0 12.9 %collective-permute-start.9 = (bf16[256,512]{1,0:T(8,128)(2,1)S(1)}, bf16[256,512]{1,0:T(8,128)(2,1)S(1)}, u32[]{:S(2)}, u32[]{:S(2)}) collective-permute-start(bf16[256,512]{1,0:T(8,128)(2,1)S(1)} %get-tuple-element.41), channel_id=1, source_target_pairs={{0,2},{1,3},{2,0},{3,1},{4,6},{5,7},{6,4},{7,5},{8,10},{9,11},{10,... | collective-permute-start | bytes 786440 | tf_op jit(solution)/shard_map/ppermute | solution.py:232
  38.2 12.4 %collective-permute-start.10 = (bf16[256,512]{1,0:T(8,128)(2,1)S(1)}, bf16[256,512]{1,0:T(8,128)(2,1)S(1)}, u32[]{:S(2)}, u32[]{:S(2)}) collective-permute-start(bf16[256,512]{1,0:T(8,128)(2,1)S(1)} %get-tuple-element.42), channel_id=1, source_target_pairs={{0,3},{1,2},{2,1},{3,0},{4,7},{5,6},{6,5},{7,4},{8,11},{9,10},{10,... | collective-permute-start | bytes 786440 | tf_op jit(solution)/shard_map/ppermute | solution.py:232
  46.7 5.6 %collective-permute-start.13 = (bf16[256,128]{1,0:T(8,128)(2,1)S(1)}, bf16[256,128]{1,0:T(8,128)(2,1)S(1)}, u32[]{:S(2)}, u32[]{:S(2)}) collective-permute-start(bf16[256,128]{1,0:T(8,128)(2,1)S(1)} %get-tuple-element.49), channel_id=1, source_target_pairs={{0,1},{1,0},{2,3},{3,2},{4,5},{5,4},{6,7},{7,6},{8,9},{9,8},{10,11... | collective-permute-start | bytes 196616 | tf_op jit(solution)/shard_map/ppermute | solution.py:232
  48.2 4.0 %collective-permute-start.14 = (bf16[256,128]{1,0:T(8,128)(2,1)S(1)}, bf16[256,128]{1,0:T(8,128)(2,1)S(1)}, u32[]{:S(2)}, u32[]{:S(2)}) collective-permute-start(bf16[256,128]{1,0:T(8,128)(2,1)S(1)} %get-tuple-element.50), channel_id=1, source_target_pairs={{0,2},{1,3},{2,0},{3,1},{4,6},{5,7},{6,4},{7,5},{8,10},{9,11},{10,... | collective-permute-start | bytes 196616 | tf_op jit(solution)/shard_map/ppermute | solution.py:232
  49.4 4.0 %collective-permute-start.15 = (bf16[256,128]{1,0:T(8,128)(2,1)S(1)}, bf16[256,128]{1,0:T(8,128)(2,1)S(1)}, u32[]{:S(2)}, u32[]{:S(2)}) collective-permute-start(bf16[256,128]{1,0:T(8,128)(2,1)S(1)} %get-tuple-element.51), channel_id=1, source_target_pairs={{0,3},{1,2},{2,1},{3,0},{4,7},{5,6},{6,5},{7,4},{8,11},{9,10},{10,... | collective-permute-start | bytes 196616 | tf_op jit(solution)/shard_map/ppermute | solution.py:232

commit v3 on v2

--- a/solution.py
+++ b/solution.py
@@ -15,6 +15,7 @@
 AXES = ("dp", "group")
 GROUPS = HEADS // KV_HEADS
 EXTRA = 16
+SKIPS = (0, 2, 4)
 
 VMEM = pl.BlockSpec(memory_space=pltpu.VMEM)
 SMEM = pl.BlockSpec(memory_space=pltpu.SMEM)
@@ -111,7 +112,7 @@
 def attend(
     tok, info, own, near, far, q0, q1, q2, q3,
     r0, r1, r2, r3, own_terms, near_terms, far_terms,
-    key_rows, value_rows, key_cols, value_cols, marks, grad_keys, grad_values,
+    key_rows, value_rows, marks, grad_keys, grad_values,
 ):
     me, quad = info[0], info[1]
     n = KV_HEADS
@@ -124,10 +125,6 @@
     value_rows[0 : 3 * tok, :] = far[3 * tok : 6 * tok, :]
     value_rows[3 * tok : 7 * tok, :] = near[4 * tok : 8 * tok, :]
     value_rows[7 * tok :, :] = own[4 * tok : 8 * tok, :]
-    for b in range(blocks):
-        at = slice(b * tok, (b + 1) * tok)
-        key_cols[:, at] = key_rows[at, :].T
-        value_cols[:, at] = value_rows[at, :].T
     for first, count, source in ((0, 3, far), (3, 4, near), (7, 4, own)):
         mark = source[source.shape[0] - EXTRA :, :].astype(F32)
         ids = mark[n : 2 * n] + 256.0 * mark[2 * n : 3 * n]
@@ -139,21 +136,22 @@
     grad_keys[...] = jnp.zeros_like(grad_keys)
     grad_values[...] = jnp.zeros_like(grad_values)
     scale = HEAD ** (-0.5)
-    key_place = lax.broadcasted_iota(jnp.int32, (span, tok), 0)
-    query_limit = before + lax.broadcasted_iota(jnp.int32, (1, tok), 1)
     mark_row = lax.broadcasted_iota(jnp.int32, (16, tok), 0)
 
-    for s, (piece, result) in enumerate(((q0, r0), (q1, r1), (q2, r2), (q3, r3))):
-        block = me ^ s
-        window = pl.ds(pl.multiple_of(block * tok, tok), span)
-        all_ids = marks[0:16, :]
+    def first_key(block):
         first = jnp.min(marks[pl.ds(block + 7, 1), :], axis=1, keepdims=True)
-        earlier = (mark_row >= block) & (mark_row < block + 7) & (all_ids < first)
-        count = jnp.sum(
+        earlier = (mark_row >= block) & (mark_row < block + 7) & (marks[0:16, :] < first)
+        return jnp.sum(
             jnp.sum(earlier.astype(F32), axis=1, keepdims=True), axis=0, keepdims=True
-        )
-        local_start = marks[pl.ds(16 + block, 1), :]
-        start = jnp.where(local_start == 0.0, count, before + local_start).astype(jnp.int32)
+        ).astype(jnp.int32)
+
+    def attend_block(block, count, piece, result, skip):
+        rows = span - skip * tok
+        window = pl.ds(pl.multiple_of((block + skip) * tok, tok), rows)
+        local_start = marks[pl.ds(16 + block, 1), :].astype(jnp.int32)
+        start = jnp.where(local_start == 0, count, before + local_start) - skip * tok
+        key_place = lax.broadcasted_iota(jnp.int32, (rows, tok), 0)
+        query_limit = before - skip * tok + lax.broadcasted_iota(jnp.int32, (1, tok), 1)
         allowed = (key_place >= start) & (key_place <= query_limit)
         bias = jnp.where(allowed, 0.0, -jnp.inf)
         bias = jnp.concatenate([bias] * GROUPS, 1)
@@ -172,7 +170,9 @@
         total = jnp.sum(weights, axis=0, keepdims=True)
         probs = weights * (1.0 / total)
         probs_low = probs.astype(BF16)
-        output = jnp.dot(value_cols[:, window], probs_low, preferred_element_type=F32)
+        output = lax.dot_general(
+            value_rows[window, :], probs_low, (((0,), (0,)), ((), ())), preferred_element_type=F32
+        )
         output = output.astype(BF16).astype(F32)
         grad_probs = lax.dot_general(
             value_rows[window, :], grad, (((1,), (1,)), ((), ())), preferred_element_type=F32
@@ -182,7 +182,9 @@
         ).astype(F32)
         delta = jnp.sum(grad_cols * output, axis=0, keepdims=True)
         grad_scores = (probs * (grad_probs - delta)).astype(BF16)
-        grad_query = jnp.dot(key_cols[:, window], grad_scores, preferred_element_type=F32)
+        grad_query = lax.dot_general(
+            key_rows[window, :], grad_scores, (((0,), (0,)), ((), ())), preferred_element_type=F32
+        )
         grad_query = grad_query * scale
         grad_values[window, :] += jnp.dot(probs_low, grad, preferred_element_type=F32)
         grad_keys[window, :] += jnp.dot(grad_scores, query, preferred_element_type=F32)
@@ -192,6 +194,17 @@
             result[0:tok, columns] = output[:, part].T.astype(BF16)
             result[tok : 2 * tok, columns] = grad_query[:, part].T.astype(BF16)
 
+    counts = [first_key(me ^ s) for s in range(n)]
+    whole = [count[0, 0] // tok for count in counts]
+    for s, (piece, result) in enumerate(((q0, r0), (q1, r1), (q2, r2), (q3, r3))):
+        for at, skip in enumerate(SKIPS):
+            fits = whole[s] >= skip
+            if at + 1 < len(SKIPS):
+                fits = fits & (whole[s] < SKIPS[at + 1])
+            pl.when(fits)(
+                functools.partial(attend_block, me ^ s, counts[s], piece, result, skip)
+            )
+
     far_terms[0 : 3 * tok, :] = (grad_keys[0 : 3 * tok, :] * scale).astype(BF16)
     far_terms[3 * tok :, :] = grad_values[0 : 3 * tok, :].astype(BF16)
     near_terms[0 : 4 * tok, :] = (grad_keys[3 * tok : 7 * tok, :] * scale).astype(BF16)
@@ -264,7 +277,9 @@
         [pltpu.VMEM((EXTRA, HEAD), F32)],
     )
     near = ring(own, n)
-    far = ring(own_late, 2 * n)
+    far = lax.ppermute(
+        own_late, AXES, [(i, i + 2 * n if i + 2 * n < count else (i + 2 * n - count) ^ n) for i in range(count)]
+    )
     blocks = 3 * n - 1
     results = call(
         functools.partial(attend, tok),
@@ -275,8 +290,6 @@
         [
             pltpu.VMEM((blocks * tok, HEAD), BF16),
             pltpu.VMEM((blocks * tok, HEAD), BF16),
-            pltpu.VMEM((HEAD, blocks * tok), BF16),
-            pltpu.VMEM((HEAD, blocks * tok), BF16),
             pltpu.VMEM((24, tok), F32),
             pltpu.VMEM((blocks * tok, HEAD), F32),
             pltpu.VMEM((blocks * tok, HEAD), F32),

time: 55.3 us -> 53.4 us (0.966)
  waiting for transfers between devices: 18 us -> 21.7 us
  starting transfers between devices: 19.6 us -> 16.7 us
  Pallas kernels: 16.4 us -> 13.8 us
    ppermute x0 -> x1, waiting for transfers between devices: none -> 12.8 us  [local(): lax.ppermute(own_late, AXES, [(i, i + 2 * n if i + 2 * n < count else i +...]
    ppermute x4 -> x3, waiting for transfers between devices: 14 us -> 5.57 us  [ring(): lax.ppermute(value, AXES, [(i, (i + steps) % count) for i in range(count)])]
    ppermute x4 -> x3, starting transfers between devices: 8.37 us -> 4.03 us  [ring(): lax.ppermute(value, AXES, [(i, (i + steps) % count) for i in range(count)])]
    pallas_call x7, Pallas kernels: 16.4 us -> 13.8 us  [call(): pl.pallas_call(kernel, out_shape=[jax.ShapeDtypeStruct(shape, dtype) for...]
    ppermute x0 -> x1, starting transfers between devices: none -> 1.3 us  [local(): lax.ppermute(own_late, AXES, [(i, i + 2 * n if i + 2 * n < count else i +...]
    ppermute x12, waiting for transfers between devices: 3.93 us -> 3.31 us  [swap(): return lax.ppermute(value, AXES, [(i, i ^ bits) for i in range(count)])]
  transfers between devices with their start and end apart: 16 -> 16, of which waited for: 5 -> 4; matrix products, arithmetic and copies ran while one was open for 0% -> 0% of each run, Pallas kernels for 9% -> 9%
where the time goes in v3:
time: 53.4 us; the launch traced here: 53.2 us
  waiting for transfers between devices  21.7 us (41%)
  starting transfers between devices  16.7 us (31%)
  Pallas kernels  13.8 us (26%)
  between operations  0.9 us (2%)
    pallas_call x7, Pallas kernels, call(): pl.pallas_call(kernel, out_shape=[jax.ShapeDtypeStruct(shape, dtype) for...  13.8 us
    ppermute x1, waiting for transfers between devices, local(): lax.ppermute(own_late, AXES, [(i, i + 2 * n if i + 2 * n < count else i +...  12.8 us
    ppermute x12, starting transfers between devices, swap(): return lax.ppermute(value, AXES, [(i, i ^ bits) for i in range(count)])  11.4 us
    ppermute x3, waiting for transfers between devices, ring(): lax.ppermute(value, AXES, [(i, (i + steps) % count) for i in range(count)])  5.57 us
    ppermute x3, starting transfers between devices, ring(): lax.ppermute(value, AXES, [(i, (i + steps) % count) for i in range(count)])  4.03 us
    ppermute x12, waiting for transfers between devices, swap(): return lax.ppermute(value, AXES, [(i, i ^ bits) for i in range(count)])  3.31 us
    ppermute x1, starting transfers between devices, local(): lax.ppermute(own_late, AXES, [(i, i + 2 * n if i + 2 * n < count else i +...  1.3 us
  transfers between devices with their start and end apart: 16, of which 4 were waited for; matrix products, arithmetic and copies ran while one was open for 0% of the time, Pallas kernels for 9%

profile of v3, /device:TPU:1, one launch (start us, length us, event | category | flops | bytes accessed | tf_op | source)
XLA Modules:
  0.0 53.2 jit_solution(1357232700601847056)
XLA Ops:
  0.7 0.1 pad_add_fusion.info
  0.7 1.5 %pack_keys.1 = (bf16[272,128]{1,0:T(8,128)(2,1)S(1)}, bf16[272,128]{1,0:T(8,128)(2,1)S(1)}, bf16[272,128]{1,0:T(8,128)(2,1)S(1)}, bf16[272,128]{1,0:T(8,128)(2,1)S(1)}) custom-call(s32[2]{0:T(128)S(1)} %pad_add_fusion.info, s32[1,128]{1,0:T(1,128)} %bitcast.3, bf16[128,512]{1,0:T(8,128)(2,1)} %keys.1, bf16[128,512]{1,0:T(8,128)(2,1)} %values.1), custom_call_target="tpu_custom_call" | custom-call | tf_op jit(solution)/shard_map/pack_keys/pallas_call | solution.py:32
  2.2 0.1 collective-permute-start
  2.4 2.7 %collective-permute-start.1 = (bf16[272,128]{1,0:T(8,128)(2,1)S(1)}, bf16[272,128]{1,0:T(8,128)(2,1)S(1)}, u32[]{:S(2)}, u32[]{:S(2)}) collective-permute-start(bf16[272,128]{1,0:T(8,128)(2,1)S(1)} %get-tuple-element.31), channel_id=1, source_target_pairs={{0,2},{1,3},{2,0},{3,1},{4,6},{5,7},{6,4},{7,5},{8,10},{9,11},{10,... | collective-permute-start | bytes 208904 | tf_op jit(solution)/shard_map/ppermute | solution.py:245
  5.0 0.0 collective-permute-start.2
  5.1 1.9 %pack_queries.1 = (bf16[272,512]{1,0:T(8,128)(2,1)S(1)}, bf16[272,512]{1,0:T(8,128)(2,1)S(1)}, bf16[272,512]{1,0:T(8,128)(2,1)S(1)}, bf16[272,512]{1,0:T(8,128)(2,1)S(1)}) custom-call(s32[2]{0:T(128)S(1)} %pad_add_fusion.info, bf16[128,2048]{1,0:T(8,128)(2,1)} %queries.1, bf16[128,2048]{1,0:T(8,128)(2,1)} %grads.1), custom_call_target="tpu_custom_call" | custom-call | tf_op jit(solution)/shard_map/pack_queries/pallas_call | solution.py:32
  7.0 0.4 collective-permute-start.5
  7.4 1.4 %collective-permute-start.6 = (bf16[272,512]{1,0:T(8,128)(2,1)S(1)}, bf16[272,512]{1,0:T(8,128)(2,1)S(1)}, u32[]{:S(2)}, u32[]{:S(2)}) collective-permute-start(bf16[272,512]{1,0:T(8,128)(2,1)S(1)} %get-tuple-element.37), channel_id=1, source_target_pairs={{0,2},{1,3},{2,0},{3,1},{4,6},{5,7},{6,4},{7,5},{8,10},{9,11},{10,... | collective-permute-start | bytes 835592 | tf_op jit(solution)/shard_map/ppermute | solution.py:245
  8.9 0.3 collective-permute-start.7
  9.2 0.0 collective-permute-done.1.s2
  9.2 0.0 collective-permute-done.2.s3
  9.2 0.6 %order_keys.1 = (bf16[1040,128]{1,0:T(8,128)(2,1)S(1)}, bf16[784,128]{1,0:T(8,128)(2,1)S(1)}) custom-call(s32[2]{0:T(128)S(1)} %pad_add_fusion.info, bf16[272,128]{1,0:T(8,128)(2,1)S(1)} %get-tuple-element.29.s0, bf16[272,128]{1,0:T(8,128)(2,1)S(1)} %collective-permute-done.s1, bf16[272,128]{1,0:T(8,128)(2,1)S(1)} %collective-permute-done.1.s2, ...), custom_call_target="tpu_custom_call" | custom-call | tf_op jit(solution)/shard_map/order_keys/pallas_call | solution.py:32
  9.8 1.7 %collective-permute-start.3 = (bf16[1040,128]{1,0:T(8,128)(2,1)S(1)}, bf16[1040,128]{1,0:T(8,128)(2,1)S(1)}, u32[]{:S(2)}, u32[]{:S(2)}) collective-permute-start(bf16[1040,128]{1,0:T(8,128)(2,1)S(1)} %get-tuple-element.33.own), channel_id=1, source_target_pairs={{0,4},{1,5},{2,6},{3,7},{4,8},{5,9},{6,10},{7,11},{8,12},{9,13},{1... | collective-permute-start | bytes 798728 | tf_op jit(solution)/shard_map/ppermute | solution.py:248
  11.5 1.3 %collective-permute-start.4 = (bf16[784,128]{1,0:T(8,128)(2,1)S(1)}, bf16[784,128]{1,0:T(8,128)(2,1)S(1)}, u32[]{:S(2)}, u32[]{:S(2)}) collective-permute-start(bf16[784,128]{1,0:T(8,128)(2,1)S(1)} %get-tuple-element.34), channel_id=1, source_target_pairs={{0,8},{1,9},{2,10},{3,11},{4,12},{5,13},{6,14},{7,15},{8,16},{9,17... | collective-permute-start | bytes 602120 | tf_op jit(solution)/shard_map/ppermute | solution.py:280
  12.8 12.8 %collective-permute-done.4.far = bf16[784,128]{1,0:T(8,128)(2,1)S(1)} collective-permute-done((bf16[784,128]{1,0:T(8,128)(2,1)S(1)}, bf16[784,128]{1,0:T(8,128)(2,1)S(1)}, u32[]{:S(2)}, u32[]{:S(2)}) %collective-permute-start.4) | collective-permute-done | bytes 200736 | tf_op jit(solution)/shard_map/ppermute | solution.py:280
  25.6 0.0 collective-permute-done.7.q3
  25.6 0.0 collective-permute-done.3.near
  25.6 6.3 %attend.1 = (bf16[256,512]{1,0:T(8,128)(2,1)S(1)}, bf16[256,512]{1,0:T(8,128)(2,1)S(1)}, bf16[256,512]{1,0:T(8,128)(2,1)S(1)}, bf16[256,512]{1,0:T(8,128)(2,1)S(...) custom-call(s32[2]{0:T(128)S(1)} %pad_add_fusion.info, ...), custom_call_target="tpu_custom_call" | custom-call | tf_op jit(solution)/shard_map/attend/pallas_call | solution.py:32
  31.9 1.7 %collective-permute-start.11 = (bf16[1024,128]{1,0:T(8,128)(2,1)S(1)}, bf16[1024,128]{1,0:T(8,128)(2,1)S(1)}, u32[]{:S(2)}, u32[]{:S(2)}) collective-permute-start(bf16[1024,128]{1,0:T(8,128)(2,1)S(1)} %get-tuple-element.46), channel_id=1, source_target_pairs={{0,28},{1,29},{2,30},{3,31},{4,0},{5,1},{6,2},{7,3},{8,4},{9,5},{1... | collective-permute-start | bytes 786440 | tf_op jit(solution)/shard_map/ppermute | solution.py:248
  33.7 1.0 %collective-permute-start.8 = (bf16[256,512]{1,0:T(8,128)(2,1)S(1)}, bf16[256,512]{1,0:T(8,128)(2,1)S(1)}, u32[]{:S(2)}, u32[]{:S(2)}) collective-permute-start(bf16[256,512]{1,0:T(8,128)(2,1)S(1)} %get-tuple-element.40), channel_id=1, source_target_pairs={{0,1},{1,0},{2,3},{3,2},{4,5},{5,4},{6,7},{7,6},{8,9},{9,8},{10,11... | collective-permute-start | bytes 786440 | tf_op jit(solution)/shard_map/ppermute | solution.py:245
  34.7 0.6 %collective-permute-start.12 = (bf16[768,128]{1,0:T(8,128)(2,1)S(1)}, bf16[768,128]{1,0:T(8,128)(2,1)S(1)}, u32[]{:S(2)}, u32[]{:S(2)}) collective-permute-start(bf16[768,128]{1,0:T(8,128)(2,1)S(1)} %get-tuple-element.47), channel_id=1, source_target_pairs={{0,24},{1,25},{2,26},{3,27},{4,28},{5,29},{6,30},{7,31},{8,0},{9,1... | collective-permute-start | bytes 589832 | tf_op jit(solution)/shard_map/ppermute | solution.py:248
  35.3 1.2 %collective-permute-start.9 = (bf16[256,512]{1,0:T(8,128)(2,1)S(1)}, bf16[256,512]{1,0:T(8,128)(2,1)S(1)}, u32[]{:S(2)}, u32[]{:S(2)}) collective-permute-start(bf16[256,512]{1,0:T(8,128)(2,1)S(1)} %get-tuple-element.41), channel_id=1, source_target_pairs={{0,2},{1,3},{2,0},{3,1},{4,6},{5,7},{6,4},{7,5},{8,10},{9,11},{10,... | collective-permute-start | bytes 786440 | tf_op jit(solution)/shard_map/ppermute | solution.py:245
  36.5 0.7 %collective-permute-start.10 = (bf16[256,512]{1,0:T(8,128)(2,1)S(1)}, bf16[256,512]{1,0:T(8,128)(2,1)S(1)}, u32[]{:S(2)}, u32[]{:S(2)}) collective-permute-start(bf16[256,512]{1,0:T(8,128)(2,1)S(1)} %get-tuple-element.42), channel_id=1, source_target_pairs={{0,3},{1,2},{2,1},{3,0},{4,7},{5,6},{6,5},{7,4},{8,11},{9,10},{10,... | collective-permute-start | bytes 786440 | tf_op jit(solution)/shard_map/ppermute | solution.py:245
  37.2 5.6 %collective-permute-done.12.far = bf16[768,128]{1,0:T(8,128)(2,1)S(1)} collective-permute-done((bf16[768,128]{1,0:T(8,128)(2,1)S(1)}, bf16[768,128]{1,0:T(8,128)(2,1)S(1)}, u32[]{:S(2)}, u32[]{:S(2)}) %collective-permute-start.12) | collective-permute-done | bytes 196640 | tf_op jit(solution)/shard_map/ppermute | solution.py:248
  42.8 0.7 %add_terms.1 = (bf16[256,128]{1,0:T(8,128)(2,1)S(1)}, bf16[256,128]{1,0:T(8,128)(2,1)S(1)}, bf16[256,128]{1,0:T(8,128)(2,1)S(1)}, bf16[256,128]{1,0:T(8,128)(2,1)S(1)}) custom-call(s32[2]{0:T(128)S(1)} %pad_add_fusion.info, f32[1024,128]{1,0:T(8,128)S(1)} %get-tuple-element.45.own, bf16[1024,128]{1,0:T(8,128)(2,1)S(1)} %collective-permute-done.11.near, ...), custom_call_target="tpu_custom_call" | custom-call | tf_op jit(solution)/shard_map/add_terms/pallas_call | solution.py:32
  43.4 1.7 %collective-permute-start.13 = (bf16[256,128]{1,0:T(8,128)(2,1)S(1)}, bf16[256,128]{1,0:T(8,128)(2,1)S(1)}, u32[]{:S(2)}, u32[]{:S(2)}) collective-permute-start(bf16[256,128]{1,0:T(8,128)(2,1)S(1)} %get-tuple-element.49), channel_id=1, source_target_pairs={{0,1},{1,0},{2,3},{3,2},{4,5},{5,4},{6,7},{7,6},{8,9},{9,8},{10,11... | collective-permute-start | bytes 196616 | tf_op jit(solution)/shard_map/ppermute | solution.py:245
  45.1 1.2 %collective-permute-start.14 = (bf16[256,128]{1,0:T(8,128)(2,1)S(1)}, bf16[256,128]{1,0:T(8,128)(2,1)S(1)}, u32[]{:S(2)}, u32[]{:S(2)}) collective-permute-start(bf16[256,128]{1,0:T(8,128)(2,1)S(1)} %get-tuple-element.50), channel_id=1, source_target_pairs={{0,2},{1,3},{2,0},{3,1},{4,6},{5,7},{6,4},{7,5},{8,10},{9,11},{10,... | collective-permute-start | bytes 196616 | tf_op jit(solution)/shard_map/ppermute | solution.py:245
  46.4 0.5 collective-permute-start.15
  46.9 2.8 %collective-permute-done.10.s3 = bf16[256,512]{1,0:T(8,128)(2,1)S(1)} collective-permute-done((bf16[256,512]{1,0:T(8,128)(2,1)S(1)}, bf16[256,512]{1,0:T(8,128)(2,1)S(1)}, u32[]{:S(2)}, u32[]{:S(2)}) %collective-permute-start.10) | collective-permute-done | bytes 262176 | tf_op jit(solution)/shard_map/ppermute | solution.py:245
  49.6 1.6 %place_queries.1 = (bf16[128,2048]{1,0:T(8,128)(2,1)}, bf16[128,2048]{1,0:T(8,128)(2,1)}) custom-call(s32[2]{0:T(128)S(1)} %pad_add_fusion.info, bf16[256,512]{1,0:T(8,128)(2,1)S(1)} %get-tuple-element.39.s0, bf16[256,512]{1,0:T(8,128)(2,1)S(1)} %collective-permute-done.8.s1, bf16[256,512]{1,0:T(8,128)(2,1)S(1)} %collective-permute-done.9.s2, ...), custom_call_target="tpu_custom_call" | custom-call | tf_op jit(solution)/shard_map/place_queries/pallas_call | solution.py:32
  51.2 0.5 collective-permute-done.15.s3
  51.7 1.3 %place_keys.1 = (bf16[128,512]{1,0:T(8,128)(2,1)}, bf16[128,512]{1,0:T(8,128)(2,1)}) custom-call(s32[2]{0:T(128)S(1)} %pad_add_fusion.info, bf16[256,128]{1,0:T(8,128)(2,1)S(1)} %get-tuple-element.48.s0, bf16[256,128]{1,0:T(8,128)(2,1)S(1)} %collective-permute-done.13.s1, bf16[256,128]{1,0:T(8,128)(2,1)S(1)} %collective-permute-done.14.s2, ...), custom_call_target="tpu_custom_call" | custom-call | tf_op jit(solution)/shard_map/place_keys/pallas_call | solution.py:32
  (8 shorter events, 0.0 us)
Async XLA Ops:
  2.2 6.6 %collective-permute-start = (bf16[272,128]{1,0:T(8,128)(2,1)S(1)}, bf16[272,128]{1,0:T(8,128)(2,1)S(1)}, u32[]{:S(2)}, u32[]{:S(2)}) collective-permute-start(bf16[272,128]{1,0:T(8,128)(2,1)S(1)} %get-tuple-element.30), channel_id=1, source_target_pairs={{0,1},{1,0},{2,3},{3,2},{4,5},{5,4},{6,7},{7,6},{8,9},{9,8},{10,11... | collective-permute-start | bytes 208904 | tf_op jit(solution)/shard_map/ppermute | solution.py:245
  2.4 6.9 %collective-permute-start.1 = (bf16[272,128]{1,0:T(8,128)(2,1)S(1)}, bf16[272,128]{1,0:T(8,128)(2,1)S(1)}, u32[]{:S(2)}, u32[]{:S(2)}) collective-permute-start(bf16[272,128]{1,0:T(8,128)(2,1)S(1)} %get-tuple-element.31), channel_id=1, source_target_pairs={{0,2},{1,3},{2,0},{3,1},{4,6},{5,7},{6,4},{7,5},{8,10},{9,11},{10,... | collective-permute-start | bytes 208904 | tf_op jit(solution)/shard_map/ppermute | solution.py:245
  5.0 4.2 %collective-permute-start.2 = (bf16[272,128]{1,0:T(8,128)(2,1)S(1)}, bf16[272,128]{1,0:T(8,128)(2,1)S(1)}, u32[]{:S(2)}, u32[]{:S(2)}) collective-permute-start(bf16[272,128]{1,0:T(8,128)(2,1)S(1)} %get-tuple-element.32), channel_id=1, source_target_pairs={{0,3},{1,2},{2,1},{3,0},{4,7},{5,6},{6,5},{7,4},{8,11},{9,10},{10,... | collective-permute-start | bytes 208904 | tf_op jit(solution)/shard_map/ppermute | solution.py:245
  7.0 18.6 %collective-permute-start.5 = (bf16[272,512]{1,0:T(8,128)(2,1)S(1)}, bf16[272,512]{1,0:T(8,128)(2,1)S(1)}, u32[]{:S(2)}, u32[]{:S(2)}) collective-permute-start(bf16[272,512]{1,0:T(8,128)(2,1)S(1)} %get-tuple-element.36), channel_id=1, source_target_pairs={{0,1},{1,0},{2,3},{3,2},{4,5},{5,4},{6,7},{7,6},{8,9},{9,8},{10,11... | collective-permute-start | bytes 835592 | tf_op jit(solution)/shard_map/ppermute | solution.py:245
  7.4 18.2 %collective-permute-start.6 = (bf16[272,512]{1,0:T(8,128)(2,1)S(1)}, bf16[272,512]{1,0:T(8,128)(2,1)S(1)}, u32[]{:S(2)}, u32[]{:S(2)}) collective-permute-start(bf16[272,512]{1,0:T(8,128)(2,1)S(1)} %get-tuple-element.37), channel_id=1, source_target_pairs={{0,2},{1,3},{2,0},{3,1},{4,6},{5,7},{6,4},{7,5},{8,10},{9,11},{10,... | collective-permute-start | bytes 835592 | tf_op jit(solution)/shard_map/ppermute | solution.py:245
  8.9 16.7 %collective-permute-start.7 = (bf16[272,512]{1,0:T(8,128)(2,1)S(1)}, bf16[272,512]{1,0:T(8,128)(2,1)S(1)}, u32[]{:S(2)}, u32[]{:S(2)}) collective-permute-start(bf16[272,512]{1,0:T(8,128)(2,1)S(1)} %get-tuple-element.38), channel_id=1, source_target_pairs={{0,3},{1,2},{2,1},{3,0},{4,7},{5,6},{6,5},{7,4},{8,11},{9,10},{10,... | collective-permute-start | bytes 835592 | tf_op jit(solution)/shard_map/ppermute | solution.py:245
  9.8 15.8 %collective-permute-start.3 = (bf16[1040,128]{1,0:T(8,128)(2,1)S(1)}, bf16[1040,128]{1,0:T(8,128)(2,1)S(1)}, u32[]{:S(2)}, u32[]{:S(2)}) collective-permute-start(bf16[1040,128]{1,0:T(8,128)(2,1)S(1)} %get-tuple-element.33.own), channel_id=1, source_target_pairs={{0,4},{1,5},{2,6},{3,7},{4,8},{5,9},{6,10},{7,11},{8,12},{9,13},{1... | collective-permute-start | bytes 798728 | tf_op jit(solution)/shard_map/ppermute | solution.py:248
  11.5 14.1 %collective-permute-start.4 = (bf16[784,128]{1,0:T(8,128)(2,1)S(1)}, bf16[784,128]{1,0:T(8,128)(2,1)S(1)}, u32[]{:S(2)}, u32[]{:S(2)}) collective-permute-start(bf16[784,128]{1,0:T(8,128)(2,1)S(1)} %get-tuple-element.34), channel_id=1, source_target_pairs={{0,8},{1,9},{2,10},{3,11},{4,12},{5,13},{6,14},{7,15},{8,16},{9,17... | collective-permute-start | bytes 602120 | tf_op jit(solution)/shard_map/ppermute | solution.py:280
  31.9 10.8 %collective-permute-start.11 = (bf16[1024,128]{1,0:T(8,128)(2,1)S(1)}, bf16[1024,128]{1,0:T(8,128)(2,1)S(1)}, u32[]{:S(2)}, u32[]{:S(2)}) collective-permute-start(bf16[1024,128]{1,0:T(8,128)(2,1)S(1)} %get-tuple-element.46), channel_id=1, source_target_pairs={{0,28},{1,29},{2,30},{3,31},{4,0},{5,1},{6,2},{7,3},{8,4},{9,5},{1... | collective-permute-start | bytes 786440 | tf_op jit(solution)/shard_map/ppermute | solution.py:248
  33.7 12.7 %collective-permute-start.8 = (bf16[256,512]{1,0:T(8,128)(2,1)S(1)}, bf16[256,512]{1,0:T(8,128)(2,1)S(1)}, u32[]{:S(2)}, u32[]{:S(2)}) collective-permute-start(bf16[256,512]{1,0:T(8,128)(2,1)S(1)} %get-tuple-element.40), channel_id=1, source_target_pairs={{0,1},{1,0},{2,3},{3,2},{4,5},{5,4},{6,7},{7,6},{8,9},{9,8},{10,11... | collective-permute-start | bytes 786440 | tf_op jit(solution)/shard_map/ppermute | solution.py:245
  34.7 8.1 %collective-permute-start.12 = (bf16[768,128]{1,0:T(8,128)(2,1)S(1)}, bf16[768,128]{1,0:T(8,128)(2,1)S(1)}, u32[]{:S(2)}, u32[]{:S(2)}) collective-permute-start(bf16[768,128]{1,0:T(8,128)(2,1)S(1)} %get-tuple-element.47), channel_id=1, source_target_pairs={{0,24},{1,25},{2,26},{3,27},{4,28},{5,29},{6,30},{7,31},{8,0},{9,1... | collective-permute-start | bytes 589832 | tf_op jit(solution)/shard_map/ppermute | solution.py:248
  35.3 11.6 %collective-permute-start.9 = (bf16[256,512]{1,0:T(8,128)(2,1)S(1)}, bf16[256,512]{1,0:T(8,128)(2,1)S(1)}, u32[]{:S(2)}, u32[]{:S(2)}) collective-permute-start(bf16[256,512]{1,0:T(8,128)(2,1)S(1)} %get-tuple-element.41), channel_id=1, source_target_pairs={{0,2},{1,3},{2,0},{3,1},{4,6},{5,7},{6,4},{7,5},{8,10},{9,11},{10,... | collective-permute-start | bytes 786440 | tf_op jit(solution)/shard_map/ppermute | solution.py:245
  36.5 13.1 %collective-permute-start.10 = (bf16[256,512]{1,0:T(8,128)(2,1)S(1)}, bf16[256,512]{1,0:T(8,128)(2,1)S(1)}, u32[]{:S(2)}, u32[]{:S(2)}) collective-permute-start(bf16[256,512]{1,0:T(8,128)(2,1)S(1)} %get-tuple-element.42), channel_id=1, source_target_pairs={{0,3},{1,2},{2,1},{3,0},{4,7},{5,6},{6,5},{7,4},{8,11},{9,10},{10,... | collective-permute-start | bytes 786440 | tf_op jit(solution)/shard_map/ppermute | solution.py:245
  43.4 7.8 %collective-permute-start.13 = (bf16[256,128]{1,0:T(8,128)(2,1)S(1)}, bf16[256,128]{1,0:T(8,128)(2,1)S(1)}, u32[]{:S(2)}, u32[]{:S(2)}) collective-permute-start(bf16[256,128]{1,0:T(8,128)(2,1)S(1)} %get-tuple-element.49), channel_id=1, source_target_pairs={{0,1},{1,0},{2,3},{3,2},{4,5},{5,4},{6,7},{7,6},{8,9},{9,8},{10,11... | collective-permute-start | bytes 196616 | tf_op jit(solution)/shard_map/ppermute | solution.py:245
  45.1 6.1 %collective-permute-start.14 = (bf16[256,128]{1,0:T(8,128)(2,1)S(1)}, bf16[256,128]{1,0:T(8,128)(2,1)S(1)}, u32[]{:S(2)}, u32[]{:S(2)}) collective-permute-start(bf16[256,128]{1,0:T(8,128)(2,1)S(1)} %get-tuple-element.50), channel_id=1, source_target_pairs={{0,2},{1,3},{2,0},{3,1},{4,6},{5,7},{6,4},{7,5},{8,10},{9,11},{10,... | collective-permute-start | bytes 196616 | tf_op jit(solution)/shard_map/ppermute | solution.py:245
  46.4 5.4 %collective-permute-start.15 = (bf16[256,128]{1,0:T(8,128)(2,1)S(1)}, bf16[256,128]{1,0:T(8,128)(2,1)S(1)}, u32[]{:S(2)}, u32[]{:S(2)}) collective-permute-start(bf16[256,128]{1,0:T(8,128)(2,1)S(1)} %get-tuple-element.51), channel_id=1, source_target_pairs={{0,3},{1,2},{2,1},{3,0},{4,7},{5,6},{6,5},{7,4},{8,11},{9,10},{10,... | collective-permute-start | bytes 196616 | tf_op jit(solution)/shard_map/ppermute | solution.py:245
